TPU v7x, 128 devices: a whole 4x4x4 slice. The times are simulated.
128 devices in a mesh: fsdp: 8 (over z, core), tp: 16 (over x, y).
Axes of the slice: x: 4, y: 4, z: 4, core: 2. Of those that a mesh axis runs over, the one named last changes fastest.
Arguments:
- momentum: float32 [8192, 14336], P('fsdp', 'tp'), may hold values from -6 to 6
- gradient: bfloat16 [8192, 14336], P('fsdp', 'tp'), may hold values from -6 to 6
- basis: float32 [14336, 512], P('tp'), may hold values from -6 to 6
Outputs:
- momentum_out: float32 [8192, 14336], P('fsdp', 'tp')
- basis_out: float32 [14336, 512], P('tp')
- update: bfloat16 [8192, 14336], P('fsdp', 'tp')
All inputs are finite; a program needn't handle non-finite values.
Results may differ from a plain program's by a relative error of at most 0.0015.
Values sent between devices are 32-bit elements; how exact they have to be, the bound alone decides.
A program may use at most 64 MiB of HBM per device.

v0:
```python
import jax
import jax.numpy as jnp
from jax import lax
from jax.sharding import PartitionSpec as P

ROWS = 8192
COLS = 14336
RANK = 512


def factor_of(gram):
    shift = 0.0001 * jnp.trace(gram) / RANK
    return jnp.linalg.cholesky(gram + shift * jnp.eye(RANK, dtype=jnp.float32))


def shards(momentum, gradient, basis):
    high = lax.Precision.HIGHEST
    buffer = momentum + gradient.astype(jnp.float32)
    inv_cols = 1.0 / jnp.sqrt(jnp.float32(COLS))
    partial_proj = jnp.dot(buffer, basis, precision=high) * inv_cols
    proj = lax.psum(partial_proj, "tp")
    gram = lax.psum(jnp.dot(proj.T, proj, precision=high), "fsdp")
    lower = factor_of(gram)
    ortho = lax.linalg.triangular_solve(lower, proj, left_side=False, lower=True, transpose_a=True)
    partial_back = lax.dot_general(buffer, ortho, (((0,), (0,)), ((), ())), precision=high)
    back = lax.psum(partial_back, "fsdp")
    sums = lax.psum(jnp.sum(back * back, axis=0), "tp")
    momentum_out = buffer - 0.05 * jnp.dot(ortho, back.T, precision=high)
    scales = jnp.sqrt(sums / COLS + 1e-06)
    basis_out = back / scales
    update = (
        jnp.sqrt(jnp.float32(ROWS) / RANK) * jnp.dot(ortho, basis_out.T, precision=high)
    ).astype(jnp.bfloat16)
    return (momentum_out, basis_out, update)


def solution(mesh):
    placed = (P("fsdp", "tp"), P("fsdp", "tp"), P("tp", None))
    return jax.shard_map(
        shards,
        mesh=mesh,
        in_specs=placed,
        out_specs=(P("fsdp", "tp"), P("tp", None), P("fsdp", "tp")),
        check_vma=False,
    )
```

profile of v0, /device:TPU:0, one launch (start us, length us, event | category | flops | bytes accessed | tf_op | source)
XLA Modules:
  0.0 506.7 jit_solution(6853349734439608868)
XLA Ops:
  8.7 9.8 %convolution_multiply_fusion = f32[1024,512]{1,0:T(8,128)} fusion(f32[896,512]{1,0:T(8,128)S(1)} %copy-done, f32[1024,896]{1,0:T(8,128)} %param.3, bf16[1024,896]{1,0:T(8,128)(2,1)} %param.4), kind=kOutput, calls=%fused_computation.7 | convolution fusion | flops 5639503872 | bytes 9437184 | tf_op jit(solution)/shard_map/dot_general | solution.py:20
  18.5 92.6 %all-reduce.5.cloned.1.call-done = f32[1024,512]{1,0:T(8,128)} async-done(((f32[1024,512]{1,0:T(8,128)}), f32[1024,512]{1,0:T(8,128)}) %all-reduce.5.cloned.1.call-update) | async-done | bytes 2097168 | tf_op jit(solution)/shard_map/psum | solution.py:21
  111.1 6.7 %fusion.39 = f32[512,512]{0,1:T(8,128)} fusion(f32[1024,512]{1,0:T(8,128)} %all-reduce.5.cloned.1.call-done), kind=kOutput, calls=%fused_computation.82 | convolution fusion | flops 3221225472 | bytes 3145728 | tf_op jit(solution)/shard_map/dot_general | solution.py:22
  118.4 61.7 %all-reduce.7.cloned.1.call-done = f32[512,512]{0,1:T(8,128)} async-done(((f32[512,512]{0,1:T(8,128)}), f32[512,512]{0,1:T(8,128)}) %all-reduce.7.cloned.1.call-update) | async-done | bytes 1048592 | tf_op jit(solution)/shard_map/psum | solution.py:22
  182.7 2.4 select_add_fusion
  185.1 2.5 copy.7
  190.0 11.7 %cholesky.103 = f32[128,128]{1,0:T(8,128)S(1)} custom-call(f32[128,128]{1,0:T(8,128)S(1)} %cholesky.263), custom_call_target="Cholesky" | custom-call | tf_op jit(solution)/shard_map/jit(cholesky)/cholesky | solution.py:13
  201.9 9.8 %custom-call.30 = f32[1,128,128]{1,2,0:T(8,128)S(1)} custom-call(f32[1,128,128]{2,1,0:T(8,128)S(1)} %get-tuple-element.30), custom_call_target="InvertDiagBlocksLowerTriangular" | custom-call | tf_op jit(solution)/shard_map/jit(cholesky)/cholesky | solution.py:13
  214.4 11.7 %cholesky.215 = f32[128,128]{1,0:T(8,128)S(1)} custom-call(f32[128,128]{1,0:T(8,128)S(1)} %cholesky.267), custom_call_target="Cholesky" | custom-call | tf_op jit(solution)/shard_map/jit(cholesky)/cholesky | solution.py:13
  226.2 10.0 %custom-call.31 = f32[1,128,128]{1,2,0:T(8,128)S(1)} custom-call(f32[1,128,128]{2,1,0:T(8,128)S(1)} %get-tuple-element.28), custom_call_target="InvertDiagBlocksLowerTriangular" | custom-call | tf_op jit(solution)/shard_map/jit(cholesky)/cholesky | solution.py:13
  238.2 11.7 %cholesky.236 = f32[128,128]{1,0:T(8,128)S(1)} custom-call(f32[128,128]{1,0:T(8,128)S(1)} %cholesky.272), custom_call_target="Cholesky" | custom-call | tf_op jit(solution)/shard_map/jit(cholesky)/cholesky | solution.py:13
  250.0 9.8 %custom-call.32 = f32[1,128,128]{1,2,0:T(8,128)S(1)} custom-call(f32[1,128,128]{2,1,0:T(8,128)S(1)} %get-tuple-element.26), custom_call_target="InvertDiagBlocksLowerTriangular" | custom-call | tf_op jit(solution)/shard_map/jit(cholesky)/cholesky | solution.py:13
  261.5 12.1 %cholesky.253 = f32[128,128]{1,0:T(8,128)S(1)} custom-call(f32[128,128]{1,0:T(8,128)S(1)} %convolution_subtract_fusion.4), custom_call_target="Cholesky" | custom-call | tf_op jit(solution)/shard_map/jit(cholesky)/cholesky | solution.py:13
  279.3 14.3 %while.1 = (s32[]{:T(128)}, f32[512,512]{0,1:T(8,128)}, s32[4,2]{0,1:T(2,128)S(1)}, f32[4,128,128]{2,1,0:T(8,128)}, s32[]{:T(128)}) while((s32[]{:T(128)}, f32[512,512]{0,1:T(8,128)}, s32[4,2]{0,1:T(2,128)S(1)}, f32[4,128,128]{2,1,0:T(8,128)}, s32[]{:T(128)}) %tuple.28), condition=%wide.while_cond, body=%wide.while_body.sunk | while | flops 2 | bytes 393329 | solution.py:24
  279.9 2.3 dynamic-slice.7
  283.5 2.3 dynamic-slice.7
  293.6 40.1 %custom-call.33 = f32[4,128,128]{1,2,0:T(8,128)S(1)} custom-call(f32[4,128,128]{2,1,0:T(8,128)} %get-tuple-element.10), custom_call_target="InvertDiagBlocksLowerTriangular" | custom-call | tf_op jit(solution)/shard_map/triangular_solve | solution.py:24
  338.4 2.8 convolution_subtract_fusion
  342.7 3.8 fusion.7
  348.7 12.9 %fusion.6 = f32[896,512]{1,0:T(8,128)} fusion(f32[1024,896]{1,0:T(8,128)S(1)} %copy-done.1, bf16[1024,896]{1,0:T(8,128)(2,1)S(1)} %copy-done.3, f32[1024,128]{0,1:T(8,128)S(1)} %fusion.24, f32[1024,128]{0,1:T(8,128)S(1)} %fusion.25, f32[1024,128]{0,1:T(8,128)S(1)} %fusion.26, f32[1024,128]{0,1:T(8,128)S(1)} %fusion.14), kind=kOutput, calls=%fused_computation.14 | convolution fusion | flops 5640552448 | bytes 9437184 | tf_op jit(solution)/shard_map/dot_general | solution.py:25
  361.7 64.4 %all-reduce.9.cloned.1.call-done = f32[896,512]{1,0:T(8,128)} async-done(((f32[896,512]{1,0:T(8,128)}), f32[896,512]{1,0:T(8,128)}) %all-reduce.9.cloned.1.call-update) | async-done | bytes 1835024 | tf_op jit(solution)/shard_map/psum | solution.py:26
  427.8 40.3 %psum.31 = f32[512]{0:T(512)S(1)} all-reduce(f32[512]{0:T(512)S(1)} %multiply_reduce_fusion), channel_id=1, replica_groups=mesh['fsdp'=8,'tp'=16] {'tp'}, use_global_device_ids=true, to_apply=%region_13.14 | all-reduce | flops 512 | bytes 4096 | tf_op jit(solution)/shard_map/psum | solution.py:27
  470.0 14.6 %multiply_convert_fusion = bf16[1024,896]{1,0:T(8,128)(2,1)} fusion(f32[896,512]{1,0:T(8,128)S(1)} %broadcast_divide_fusion, f32[1024,128]{0,1:T(8,128)S(1)} %copy-done.9, f32[1024,128]{0,1:T(8,128)S(1)} %fusion.25, f32[1024,128]{0,1:T(8,128)S(1)} %fusion.26, f32[1024,128]{0,1:T(8,128)S(1)} %fusion.14), kind=kOutput, calls=%fused_computation.2 | convolution fusion | flops 5640552448 | bytes 5767168 | tf_op jit(solution)/shard_map/dot_general | solution.py:32
  484.6 15.4 %multiply_subtract_fusion = f32[1024,896]{1,0:T(8,128)} fusion(f32[896,512]{1,0:T(8,128)S(1)} %copy-done.6, f32[1024,896]{1,0:T(8,128)S(1)} %copy-done.2, bf16[1024,896]{1,0:T(8,128)(2,1)S(1)} %copy-done.4, f32[1024,128]{0,1:T(8,128)S(1)} %copy-done.9, f32[1024,128]{0,1:T(8,128)S(1)} %fusion.25, f32[1024,128]{0,1:T(8,128)S(1)} %fusion.26, ...), kind=kOutput, calls=%fused_computation.3 | convolution fusion | flops 5642387456 | bytes 13107200 | tf_op jit(solution)/shard_map/dot_general | solution.py:28
  (90 shorter events, 37.7 us)
Async XLA Ops:
  7.2 1.5 copy-start
  7.2 103.9 %all-reduce.5.cloned.1.call-start = ((), (), s32[]{:S(2)}) async-start(), calls=%async_computation | async-start | bytes 4194304 | tf_op jit(solution)/shard_map/psum | solution.py:21
  18.5 161.6 %all-reduce.7.cloned.1.call-start = ((), (), s32[]{:S(2)}) async-start(), calls=%async_computation.1 | async-start | bytes 2097152 | tf_op jit(solution)/shard_map/psum | solution.py:22
  117.9 308.2 %all-reduce.9.cloned.1.call-start = ((), (), s32[]{:S(2)}) async-start(), calls=%async_computation.2 | async-start | bytes 3670016 | tf_op jit(solution)/shard_map/psum | solution.py:26
  182.6 4.9 copy-start.7
  189.0 1.0 copy-start.10
  333.8 4.6 copy-start.12
  333.8 4.6 copy-start.5
  338.3 10.4 %copy-start.3 = (bf16[1024,896]{1,0:T(8,128)(2,1)S(1)}, bf16[1024,896]{1,0:T(8,128)(2,1)}, u32[]{:S(2)}) copy-start(bf16[1024,896]{1,0:T(8,128)(2,1)} %param.4) | copy-start | bytes 5505028
  342.7 6.0 %copy-start.1 = (f32[1024,896]{1,0:T(8,128)S(1)}, f32[1024,896]{1,0:T(8,128)}, u32[]{:S(2)}) copy-start(f32[1024,896]{1,0:T(8,128)} %param.3) | copy-start | bytes 11010052
  347.9 0.8 copy-start.8
  468.1 1.8 copy-start.9
  469.9 14.7 %copy-start.11 = (f32[896,512]{1,0:T(8,128)}, f32[896,512]{1,0:T(8,128)S(1)}, u32[]{:S(2)}) copy-start(f32[896,512]{1,0:T(8,128)S(1)} %broadcast_divide_fusion) | copy-start | bytes 5505028
  469.9 14.6 %copy-start.2 = (f32[1024,896]{1,0:T(8,128)S(1)}, f32[1024,896]{1,0:T(8,128)}, u32[]{:S(2)}) copy-start(f32[1024,896]{1,0:T(8,128)} %param.3) | copy-start | bytes 11010052
  469.9 14.6 %copy-start.4 = (bf16[1024,896]{1,0:T(8,128)(2,1)S(1)}, bf16[1024,896]{1,0:T(8,128)(2,1)}, u32[]{:S(2)}) copy-start(bf16[1024,896]{1,0:T(8,128)(2,1)} %param.4) | copy-start | bytes 5505028
  469.9 14.6 %copy-start.6 = (f32[896,512]{1,0:T(8,128)S(1)}, f32[896,512]{1,0:T(8,128)}, u32[]{:S(2)}) copy-start(f32[896,512]{1,0:T(8,128)} %all-reduce.9.cloned.1.call-done) | copy-start | bytes 5505028
Sparse Core Ops, SparseCore 0:
  18.6 92.4 all-reduce.4
  118.0 62.0 all-reduce.6
  361.8 64.2 all-reduce.8
where the time goes:
time: 513 us; the launch traced here: 507 us
  waiting for transfers between devices  219 us (43%)
  other arithmetic  129 us (25%)
  matrix products  79.3 us (15%)
  blocking collectives  40.3 us (8%)
  local copies, waits for them, and re-layouts  20.7 us (4%)
  between operations  17.6 us (3%)
    psum x1, waiting for transfers between devices, shards(): proj = lax.psum(partial_proj, 'tp')  92.6 us
    another operation x14, other arithmetic, factor_of(): return jnp.linalg.cholesky(gram + shift * jnp.eye(RANK, dtype=jnp.float32))  78.9 us
    psum x1, waiting for transfers between devices, shards(): back = lax.psum(partial_back, 'fsdp')  64.4 us
    psum x1, waiting for transfers between devices, shards(): gram = lax.psum(jnp.dot(proj.T, proj, precision=high), 'fsdp')  61.7 us
    another operation x3, other arithmetic, shards(): lax.linalg.triangular_solve(lower, proj, left_side=False, lower=True, tra...  41.2 us
    psum x1, blocking collectives, shards(): sums = lax.psum(jnp.sum(back * back, axis=0), 'tp')  40.3 us
    dot_general x1, matrix products, shards(): momentum_out = buffer - 0.05 * jnp.dot(ortho, back.T, precision=high)  15.4 us
    dot_general x1, matrix products, shards(): jnp.dot(ortho, basis_out.T, precision=high)  14.6 us
  transfers between devices with their start and end apart: 3, of which 3 were waited for; matrix products, arithmetic and copies ran while one was open for 0% of the time, Pallas kernels for 0%

commit v1 on v0

--- a/solution.py
+++ b/solution.py
@@ -1,16 +1,109 @@
-import jax
-import jax.numpy as jnp
+import jax, jax.numpy as jnp
 from jax import lax
+from jax.experimental import pallas as pl
+from jax.experimental.pallas import tpu as pltpu
 from jax.sharding import PartitionSpec as P
+
+def lane(v, j, mode):
+    if mode == 0:
+        return jnp.broadcast_to(v[:, j:j+1], v.shape)
+    return jnp.take_along_axis(v, jnp.full(v.shape, j, jnp.int32), axis=1)
+
+def sub(v, j, mode):
+    if mode == 0:
+        return jnp.broadcast_to(v[j:j+1, :], v.shape)
+    return jnp.take_along_axis(v, jnp.full(v.shape, j, jnp.int32), axis=0)
+
+def chol_inv_128(g, mode=0, n=16):
+    sid = lax.broadcasted_iota(jnp.int32, (8, 128), 0)
+    lid = lax.broadcasted_iota(jnp.int32, (8, 128), 1)
+    x = [jnp.where(lid == sid + 8 * s, 1.0, 0.0).astype(jnp.float32) for s in range(n)]
+    out = []
+    for s in range(n):
+        P, Q = g[s], x[s]
+        look = s + 1 < n
+        cb = [lane(P, 8 * s + j, mode) for j in range(8)]
+        if look:
+            N, NX = g[s + 1], x[s + 1]
+            cn = [lane(N, 8 * s + j, mode) for j in range(8)]
+        for j in range(8):
+            d = 1.0 / sub(cb[j], j, mode)
+            cm = jnp.where(sid > j, cb[j], 0.0)
+            for k in range(j + 1, 8):
+                m = sub(cb[k], j, mode) * d
+                cb[k] = cb[k] - cm * m
+                if look:
+                    cn[k] = cn[k] - cn[j] * m
+            u, ux = sub(P, j, mode) * d, sub(Q, j, mode) * d
+            P, Q = P - cm * u, Q - cm * ux
+            if look:
+                N, NX = N - cn[j] * u, NX - cn[j] * ux
+        pv = cb[0]
+        for j in range(1, 8):
+            pv = jnp.where(sid == j, cb[j], pv)
+        r = lax.rsqrt(pv)
+        R, RX = P * r, Q * r
+        out.append(RX)
+        if look:
+            g[s + 1], x[s + 1] = N, NX
+        if s + 2 < n:
+            T = R.T
+            rb = [sub(R, j, mode) for j in range(8)]
+            rxb = [sub(RX, j, mode) for j in range(8)]
+            for i in range(s + 2, n):
+                Ti = T[8 * i:8 * i + 8, :]
+                gi, xi = g[i], x[i]
+                for j in range(8):
+                    l = jnp.broadcast_to(Ti[:, j:j+1], (8, 128))
+                    gi = gi - l * rb[j]
+                    xi = xi - l * rxb[j]
+                g[i], x[i] = gi, xi
+    return out
+
+HI = lax.Precision.HIGHEST
+
+def chol_kernel(mode, g_ref, x_ref, s_ref, d_ref):
+    n = g_ref.shape[0]
+    nb = n // 128
+    rid = lax.broadcasted_iota(jnp.int32, (n, n), 0)
+    cid = lax.broadcasted_iota(jnp.int32, (n, n), 1)
+    G = g_ref[...]
+    eye = jnp.where(rid == cid, 1.0, 0.0)
+    shift = jnp.sum(G * eye) * (0.0001 / n)
+    s_ref[...] = G + shift * eye
+
+    def step(k, c):
+        o = pl.multiple_of(k * 128, 128)
+        tiles = [s_ref[pl.ds(o + 8 * i, 8), pl.ds(o, 128)] for i in range(16)]
+        out = chol_inv_128(tiles, mode)
+        for i in range(16):
+            d_ref[8 * i:8 * i + 8, :] = out[i]
+        e128 = jnp.where(lax.broadcasted_iota(jnp.int32, (128, 128), 0) == lax.broadcasted_iota(jnp.int32, (128, 128), 1), 1.0, 0.0).astype(jnp.float32)
+        s_ref[pl.ds(o, 128), pl.ds(o, 128)] = e128
+        R = jnp.dot(d_ref[...], s_ref[pl.ds(o, 128), :], precision=HI, preferred_element_type=jnp.float32)
+        s_ref[pl.ds(o, 128), :] = R
+        def row(i, c):
+            oi = pl.multiple_of(i * 128, 128)
+            L = s_ref[pl.ds(o, 128), pl.ds(oi, 128)]
+            s_ref[pl.ds(oi, 128), pl.ds(o, 128)] = jnp.zeros((128, 128), jnp.float32)
+            s_ref[pl.ds(oi, 128), :] -= lax.dot_general(L, s_ref[pl.ds(o, 128), :], (((0,), (0,)), ((), ())), precision=HI, preferred_element_type=jnp.float32)
+            return c
+        lax.fori_loop(k + 1, nb, row, 0)
+        return c
+    lax.fori_loop(0, nb, step, 0)
+    x_ref[...] = jnp.where(cid <= rid, s_ref[...], 0.0)
+
+def chol_inv(G, mode=0, **kw):
+    n = G.shape[0]
+    return pl.pallas_call(
+        lambda *a: chol_kernel(mode, *a),
+        out_shape=jax.ShapeDtypeStruct((n, n), jnp.float32),
+        scratch_shapes=[pltpu.VMEM((n, n), jnp.float32), pltpu.VMEM((128, 128), jnp.float32)],
+        compiler_params=pltpu.CompilerParams(vmem_limit_bytes=50 * 2**20), **kw)(G)
 
 ROWS = 8192
 COLS = 14336
 RANK = 512
-
-
-def factor_of(gram):
-    shift = 0.0001 * jnp.trace(gram) / RANK
-    return jnp.linalg.cholesky(gram + shift * jnp.eye(RANK, dtype=jnp.float32))
 
 
 def shards(momentum, gradient, basis):
@@ -20,8 +113,8 @@
     partial_proj = jnp.dot(buffer, basis, precision=high) * inv_cols
     proj = lax.psum(partial_proj, "tp")
     gram = lax.psum(jnp.dot(proj.T, proj, precision=high), "fsdp")
-    lower = factor_of(gram)
-    ortho = lax.linalg.triangular_solve(lower, proj, left_side=False, lower=True, transpose_a=True)
+    inverse = chol_inv(gram, 1)
+    ortho = jnp.dot(proj, inverse.T, precision=high)
     partial_back = lax.dot_general(buffer, ortho, (((0,), (0,)), ((), ())), precision=high)
     back = lax.psum(partial_back, "fsdp")
     sums = lax.psum(jnp.sum(back * back, axis=0), "tp")

time: 513 us -> 349 us (0.68); the launches traced: 507 us -> 349 us
  other arithmetic: 129 us -> 3.6 us
  matrix products: 79.3 us -> 45.7 us
  Pallas kernels: 0 us -> 22 us
  local copies, waits for them, and re-layouts: 20.7 us -> 4.23 us
    another operation x17 -> x0, other arithmetic: 120 us -> none  [the longest x14 78.9 us: factor_of(): return jnp.linalg.cholesky(gram + shift * jnp.eye(RANK, dtype=jnp.float32))]
    pallas_call x0 -> x1, Pallas kernels: none -> 22 us  [chol_inv(): pl.pallas_call(lambda *a: chol_kernel(mode, *a), out_shape=jax.ShapeDtype...]
    another operation x13 -> x0, matrix products: 20 us -> none  [the longest x7 14 us: shards(): lax.linalg.triangular_solve(lower, proj, left_side=False, lower=True, tra...]
    another operation x34 -> x0, local copies, waits for them, and re-layouts: 15 us -> none
    dot_general x1, matrix products: 14.6 us -> 8.03 us  [shards(): jnp.dot(ortho, basis_out.T, precision=high)]
    dot_general x1, matrix products: 15.4 us -> 8.79 us  [shards(): momentum_out = buffer - 0.05 * jnp.dot(ortho, back.T, precision=high)]
    dot_general x1, matrix products: 12.9 us -> 7.24 us  [shards(): lax.dot_general(buffer, ortho, (((0,), (0,)), ((), ())), precision=high)]
    dot_general x0 -> x1, matrix products: none -> 5.22 us  [shards(): ortho = jnp.dot(proj, inverse.T, precision=high)]
where the time goes in v1:
time: 349 us
  waiting for transfers between devices  219 us (63%)
  matrix products  45.7 us (13%)
  blocking collectives  40.3 us (12%)
  Pallas kernels  22 us (6%)
  between operations  13.8 us (4%)
  local copies, waits for them, and re-layouts  4.23 us (1%)
  other arithmetic  3.6 us (1%)
    psum x1, waiting for transfers between devices, shards(): proj = lax.psum(partial_proj, 'tp')  92.6 us
    psum x1, waiting for transfers between devices, shards(): back = lax.psum(partial_back, 'fsdp')  64.4 us
    psum x1, waiting for transfers between devices, shards(): gram = lax.psum(jnp.dot(proj.T, proj, precision=high), 'fsdp')  62.2 us
    psum x1, blocking collectives, shards(): sums = lax.psum(jnp.sum(back * back, axis=0), 'tp')  40.3 us
    pallas_call x1, Pallas kernels, chol_inv(): pl.pallas_call(lambda *a: chol_kernel(mode, *a), out_shape=jax.ShapeDtype...  22 us
    dot_general x1, matrix products, shards(): partial_proj = jnp.dot(buffer, basis, precision=high) * inv_cols  9.76 us
    dot_general x1, matrix products, shards(): momentum_out = buffer - 0.05 * jnp.dot(ortho, back.T, precision=high)  8.79 us
    dot_general x1, matrix products, shards(): jnp.dot(ortho, basis_out.T, precision=high)  8.03 us
  transfers between devices with their start and end apart: 3, of which 3 were waited for; matrix products, arithmetic and copies ran while one was open for 0% of the time, Pallas kernels for 0%

profile of v1, /device:TPU:0, one launch (start us, length us, event | category | flops | bytes accessed | tf_op | source)
XLA Modules:
  0.0 349.1 jit_solution(7179168915757926373)
XLA Ops:
  7.2 0.0 copy-start
  7.2 0.0 all-reduce.4.cloned.1.call-start
  7.2 1.4 copy-done
  8.7 9.8 %convolution_multiply_fusion = f32[1024,512]{1,0:T(8,128)} fusion(f32[896,512]{1,0:T(8,128)S(1)} %copy-done, f32[1024,896]{1,0:T(8,128)} %param.3, bf16[1024,896]{1,0:T(8,128)(2,1)} %param.4), kind=kOutput, calls=%fused_computation.4 | convolution fusion | flops 5639503872 | bytes 9437184 | tf_op jit(solution)/shard_map/dot_general | solution.py:113
  18.4 0.0 all-reduce.4.cloned.1.call-update
  18.5 0.0 all-reduce.6.cloned.1.call-start
  18.5 92.6 %all-reduce.4.cloned.1.call-done = f32[1024,512]{1,0:T(8,128)} async-done(((f32[1024,512]{1,0:T(8,128)}), f32[1024,512]{1,0:T(8,128)}) %all-reduce.4.cloned.1.call-update) | async-done | bytes 2097168 | tf_op jit(solution)/shard_map/psum | solution.py:114
  111.1 6.7 %fusion.1 = f32[512,512]{1,0:T(8,128)} fusion(f32[1024,512]{1,0:T(8,128)} %all-reduce.4.cloned.1.call-done), kind=kOutput, calls=%fused_computation.8 | convolution fusion | flops 3221225472 | bytes 3145728 | tf_op jit(solution)/shard_map/dot_general | solution.py:115
  117.8 0.0 all-reduce.6.cloned.1.call-update
  117.8 0.0 all-reduce.8.cloned.1.call-start
  117.9 62.2 %all-reduce.6.cloned.1.call-done.a_0_ = f32[512,512]{1,0:T(8,128)} async-done(((f32[512,512]{1,0:T(8,128)}), f32[512,512]{1,0:T(8,128)}) %all-reduce.6.cloned.1.call-update) | async-done | bytes 1048592 | tf_op jit(solution)/shard_map/psum | solution.py:115
  180.1 1.2 copy-done.1
  181.3 22.0 %shard_map.58 = f32[512,512]{1,0:T(8,128)S(1)} custom-call(f32[512,512]{1,0:T(8,128)S(1)} %copy-done.1), custom_call_target="tpu_custom_call" | custom-call | tf_op jit(solution)/shard_map/pallas_call | solution.py:98
  203.4 5.2 %fusion.2 = f32[1024,512]{1,0:T(8,128)S(1)} fusion(f32[1024,512]{1,0:T(8,128)} %all-reduce.4.cloned.1.call-done, f32[512,512]{1,0:T(8,128)S(1)} %shard_map.58), kind=kOutput, calls=%fused_computation.9 | convolution fusion | flops 3221225472 | bytes 5242880 | tf_op jit(solution)/shard_map/dot_general | solution.py:117
  208.6 1.3 copy-done.4
  209.9 7.2 %fusion = f32[896,512]{1,0:T(8,128)} fusion(f32[1024,512]{1,0:T(8,128)S(1)} %fusion.2, f32[1024,896]{1,0:T(8,128)S(1)} %copy-done.2, bf16[1024,896]{1,0:T(8,128)(2,1)S(1)} %copy-done.6), kind=kOutput, calls=%fused_computation.5 | convolution fusion | flops 5638979584 | bytes 9437184 | tf_op jit(solution)/shard_map/dot_general | solution.py:118
  217.2 0.0 all-reduce.8.cloned.1.call-update
  217.2 64.4 %all-reduce.8.cloned.1.call-done = f32[896,512]{1,0:T(8,128)} async-done(((f32[896,512]{1,0:T(8,128)}), f32[896,512]{1,0:T(8,128)}) %all-reduce.8.cloned.1.call-update) | async-done | bytes 1835024 | tf_op jit(solution)/shard_map/psum | solution.py:119
  281.6 1.7 multiply_reduce_fusion
  283.3 40.3 %psum.31 = f32[512]{0:T(512)S(1)} all-reduce(f32[512]{0:T(512)S(1)} %multiply_reduce_fusion), channel_id=1, replica_groups=mesh['fsdp'=8,'tp'=16] {'tp'}, use_global_device_ids=true, to_apply=%region_4.0 | all-reduce | flops 512 | bytes 4096 | tf_op jit(solution)/shard_map/psum | solution.py:120
  323.6 1.9 broadcast_divide_fusion
  325.5 0.2 copy-done.5
  325.7 8.0 %multiply_convert_fusion = bf16[1024,896]{1,0:T(8,128)(2,1)} fusion(f32[1024,512]{1,0:T(8,128)S(1)} %copy-done.5, f32[896,512]{1,0:T(8,128)S(1)} %broadcast_divide_fusion), kind=kOutput, calls=%fused_computation | convolution fusion | flops 5638979584 | bytes 5767168 | tf_op jit(solution)/shard_map/dot_general | solution.py:125
  333.8 8.8 %multiply_subtract_fusion = f32[1024,896]{1,0:T(8,128)} fusion(f32[1024,512]{1,0:T(8,128)S(1)} %copy-done.5, f32[896,512]{1,0:T(8,128)S(1)} %copy-done.8, f32[1024,896]{1,0:T(8,128)S(1)} %copy-done.3, bf16[1024,896]{1,0:T(8,128)(2,1)S(1)} %copy-done.7), kind=kOutput, calls=%fused_computation.1 | convolution fusion | flops 5640814592 | bytes 13107200 | tf_op jit(solution)/shard_map/dot_general | solution.py:121
  (16 shorter events, 0.0 us)
Async XLA Ops:
  7.2 1.5 copy-start
  7.2 103.9 %all-reduce.4.cloned.1.call-start = ((), (), s32[]{:S(2)}) async-start(), calls=%async_computation | async-start | bytes 4194304 | tf_op jit(solution)/shard_map/psum | solution.py:114
  18.5 161.6 %all-reduce.6.cloned.1.call-start = ((), (), s32[]{:S(2)}) async-start(), calls=%async_computation.1 | async-start | bytes 2097152 | tf_op jit(solution)/shard_map/psum | solution.py:115
  117.8 163.7 %all-reduce.8.cloned.1.call-start = ((), (), s32[]{:S(2)}) async-start(), calls=%async_computation.2 | async-start | bytes 3670016 | tf_op jit(solution)/shard_map/psum | solution.py:119
  180.1 1.2 copy-start.1
  181.3 28.6 %copy-start.6 = (bf16[1024,896]{1,0:T(8,128)(2,1)S(1)}, bf16[1024,896]{1,0:T(8,128)(2,1)}, u32[]{:S(2)}) copy-start(bf16[1024,896]{1,0:T(8,128)(2,1)} %param.4) | copy-start | bytes 5505028
  203.3 6.6 %copy-start.2 = (f32[1024,896]{1,0:T(8,128)S(1)}, f32[1024,896]{1,0:T(8,128)}, u32[]{:S(2)}) copy-start(f32[1024,896]{1,0:T(8,128)} %param.3) | copy-start | bytes 11010052
  208.6 1.3 copy-start.4
  323.6 2.1 copy-start.5
  323.6 10.2 %copy-start.8 = (f32[896,512]{1,0:T(8,128)S(1)}, f32[896,512]{1,0:T(8,128)}, u32[]{:S(2)}) copy-start(f32[896,512]{1,0:T(8,128)} %all-reduce.8.cloned.1.call-done) | copy-start | bytes 5505028
  325.7 8.0 %copy-start.9 = (f32[896,512]{1,0:T(8,128)}, f32[896,512]{1,0:T(8,128)S(1)}, u32[]{:S(2)}) copy-start(f32[896,512]{1,0:T(8,128)S(1)} %broadcast_divide_fusion) | copy-start | bytes 5505028
  325.7 8.0 %copy-start.3 = (f32[1024,896]{1,0:T(8,128)S(1)}, f32[1024,896]{1,0:T(8,128)}, u32[]{:S(2)}) copy-start(f32[1024,896]{1,0:T(8,128)} %param.3) | copy-start | bytes 11010052
  325.7 8.0 %copy-start.7 = (bf16[1024,896]{1,0:T(8,128)(2,1)S(1)}, bf16[1024,896]{1,0:T(8,128)(2,1)}, u32[]{:S(2)}) copy-start(bf16[1024,896]{1,0:T(8,128)(2,1)} %param.4) | copy-start | bytes 5505028
Sparse Core Ops, SparseCore 0:
  18.6 92.4 all-reduce.3
  117.9 62.0 all-reduce.5
  217.3 64.2 all-reduce.7

commit v2 on v0

v2 whole, which is shorter than its diff:
```python
import functools

import jax
import jax.numpy as jnp
from jax import lax
from jax.experimental import pallas as pl
from jax.experimental.pallas import tpu as pltpu
from jax.sharding import PartitionSpec as P

ROWS = 8192
COLS = 14336
RANK = 512
HI = lax.Precision.HIGHEST
F32 = jnp.float32
BF16 = jnp.bfloat16
MESH = pl.DeviceIdType.MESH
NT = (((1,), (1,)), ((), ()))
TN = (((0,), (0,)), ((), ()))
NN = (((1,), (0,)), ((), ()))


def split(v):
    high = v.astype(BF16)
    return high, (v - high.astype(F32)).astype(BF16)


def dot3(ah, al, bh, bl, dims=NN):
    def one(a, b):
        return lax.dot_general(a, b, dims, preferred_element_type=F32)

    return one(ah, bl) + one(al, bh) + one(ah, bh)


class Links:
    def __init__(self, send_sem, recv_sem):
        self.send_sem, self.recv_sem, self.used, self.sent = send_sem, recv_sem, 0, []

    def slot(self):
        self.used += 1
        return self.used - 1

    def copy(self, slot, src, dst, device):
        return pltpu.make_async_remote_copy(
            src_ref=src,
            dst_ref=dst,
            send_sem=self.send_sem.at[slot],
            recv_sem=self.recv_sem.at[slot],
            device_id=device,
            device_id_type=MESH,
        )

    def send(self, slot, src, dst, device):
        c = self.copy(slot, src, dst, device)
        c.start()
        self.sent.append(c)

    def landed(self, slot, dst, device):
        self.copy(slot, dst, dst, device).wait_recv()

    def drain(self):
        for c in self.sent:
            c.wait_send()


class Ring:
    def __init__(self, me, at):
        self.me = me
        self.r, self.l, self.o = lax.rem(me + 1, 4), lax.rem(me + 3, 4), lax.rem(me + 2, 4)
        self.right, self.left, self.far = at(self.r), at(self.l), at(self.o)


class Reduce:
    def __init__(self, links, ring, ref, base, rows, land):
        self.k, self.g, self.ref, self.base, self.rows, self.land = links, ring, ref, base, rows, land
        self.s = [links.slot() for _ in range(6)]

    def half(self, chunk, h):
        n = self.rows // 2
        return self.ref.at[pl.ds(pl.multiple_of(self.base + chunk * self.rows + h * n, n), n), :]

    def relay(self):
        self.k.send(self.s[0], self.half(self.g.o, 0), self.land.at[0], self.g.right)
        self.k.send(self.s[1], self.half(self.g.o, 1), self.land.at[1], self.g.left)

    def direct(self):
        self.k.send(self.s[2], self.half(self.g.r, 1), self.land.at[2], self.g.right)
        self.k.send(self.s[3], self.half(self.g.l, 0), self.land.at[3], self.g.left)

    def mid(self):
        for d, (chunk, device) in enumerate(((self.g.r, self.g.right), (self.g.l, self.g.left))):
            self.k.landed(self.s[d], self.land.at[d], device)
            part = self.half(chunk, d)
            part[...] += self.land[d]
            self.k.send(self.s[4 + d], part, self.land.at[4 + d], device)

    def finish(self):
        for d in range(2, 6):
            self.k.landed(self.s[d], self.land.at[d], self.g.right)
        first = self.half(self.g.me, 0)[...] + self.land[4] + self.land[3]
        second = self.half(self.g.me, 1)[...] + self.land[5] + self.land[2]
        return first, second


class Gather:
    def __init__(self, links, ring, ref, base, rows):
        self.k, self.g, self.ref, self.base, self.rows = links, ring, ref, base, rows
        self.s = [links.slot() for _ in range(4)]

    def chunk(self, i):
        return self.ref.at[pl.ds(pl.multiple_of(self.base + i * self.rows, self.rows), self.rows), :]

    def half(self, i, h):
        n = self.rows // 2
        return self.ref.at[pl.ds(pl.multiple_of(self.base + i * self.rows + h * n, n), n), :]

    def start(self):
        own = self.chunk(self.g.me)
        self.k.send(self.s[0], own, own, self.g.right)
        self.k.send(self.s[1], own, own, self.g.left)

    def mid(self):
        self.k.landed(self.s[0], self.chunk(self.g.l), self.g.right)
        part = self.half(self.g.l, 0)
        self.k.send(self.s[2], part, part, self.g.right)
        self.k.landed(self.s[1], self.chunk(self.g.r), self.g.left)
        part = self.half(self.g.r, 1)
        self.k.send(self.s[3], part, part, self.g.left)

    def finish(self):
        self.k.landed(self.s[2], self.half(self.g.o, 0), self.g.right)
        self.k.landed(self.s[3], self.half(self.g.o, 1), self.g.left)


class SumOver8:
    def __init__(self, links, ring, core, partner, ref, pair, land, total):
        self.k, self.core, self.partner, self.ref, self.pair, self.total = links, core, partner, ref, pair, total
        self.ring = ring
        self.n = ref.shape[0] // 2
        self.s = [links.slot() for _ in range(5)]
        self.base = pl.multiple_of(core * self.n, self.n)
        self.other = pl.multiple_of((1 - core) * self.n, self.n)
        self.reduce = Reduce(links, ring, ref, self.base, self.n // 4, land)
        self.gather = Gather(links, ring, total, self.base, self.n // 4)

    def exchange(self):
        self.k.send(self.s[0], self.ref.at[pl.ds(self.other, self.n), :], self.pair, self.partner)

    def begin(self):
        self.k.landed(self.s[0], self.pair, self.partner)
        self.ref[pl.ds(self.base, self.n), :] += self.pair[...]
        self.reduce.relay()
        self.reduce.direct()

    def mid(self):
        self.reduce.mid()

    def pass_on(self, j, chunk):
        part = self.gather.chunk(chunk)
        self.k.send(self.s[1 + j], part, part, self.partner)

    def turn(self):
        first, second = self.reduce.finish()
        self.gather.half(self.ring.me, 0)[...] = first
        self.gather.half(self.ring.me, 1)[...] = second
        self.gather.start()
        self.pass_on(0, self.ring.me)

    def forward(self):
        self.gather.mid()
        self.pass_on(1, self.ring.l)
        self.pass_on(2, self.ring.r)

    def last(self):
        self.gather.finish()
        self.pass_on(3, self.ring.o)

    def end(self):
        rows = self.n // 4
        for j, chunk in enumerate((self.ring.me, self.ring.l, self.ring.r, self.ring.o)):
            at = pl.multiple_of(self.other + chunk * rows, rows)
            self.k.landed(self.s[1 + j], self.total.at[pl.ds(at, rows), :], self.partner)


def lane(v, j):
    return jnp.take_along_axis(v, jnp.full(v.shape, j, jnp.int32), axis=1)


def row(v, j):
    return jnp.broadcast_to(v[j:j + 1, :], v.shape)


def eight(s, a_ref, r_ref, t_ref):
    sid = lax.broadcasted_iota(jnp.int32, (8, 128), 0)
    o = pl.multiple_of(8 * s, 8)
    on = pl.multiple_of(8 * s + 8, 8)
    p, q = a_ref[pl.ds(o, 8), 0:128], a_ref[pl.ds(o, 8), 128:256]
    n, nx = a_ref[pl.ds(on, 8), 0:128], a_ref[pl.ds(on, 8), 128:256]
    last = r_ref[...]
    t = t_ref[pl.ds(on, 8), :]
    for j in range(8):
        l = jnp.broadcast_to(t[:, j:j + 1], (8, 128))
        n = n - l * row(last[:, 0:128], j)
        nx = nx - l * row(last[:, 128:256], j)
    cb = [lane(p, 8 * s + j) for j in range(8)]
    cn = [lane(n, 8 * s + j) for j in range(8)]
    for j in range(8):
        d = 1.0 / row(cb[j], j)
        cm = jnp.where(sid > j, cb[j], 0.0)
        for k in range(j + 1, 8):
            m = row(cb[k], j) * d
            cb[k] = cb[k] - cm * m
            cn[k] = cn[k] - cn[j] * m
        u, ux = row(p, j) * d, row(q, j) * d
        p, q = p - cm * u, q - cm * ux
        n, nx = n - cn[j] * u, nx - cn[j] * ux
    pivots = cb[0]
    for j in range(1, 8):
        pivots = jnp.where(sid == j, cb[j], pivots)
    scale = lax.rsqrt(pivots)
    p, q = p * scale, q * scale
    rest = jnp.dot(t_ref[0:128, :], last, precision=HI, preferred_element_type=F32)
    rid = lax.broadcasted_iota(jnp.int32, (128, 256), 0)
    a_ref[0:128, :] -= jnp.where(rid >= 8 * s + 16, rest, 0.0)
    a_ref[pl.ds(o, 8), 128:256] = q
    a_ref[pl.ds(on, 8), 0:128] = n
    a_ref[pl.ds(on, 8), 128:256] = nx
    r_ref[:, 0:128] = p
    r_ref[:, 128:256] = q
    t_ref[0:128, :] = p.T


def factor_step(k, s_ref, a_ref, r_ref, t_ref, event):
    n = s_ref.shape[0]
    o = 128 * k
    i128 = lax.broadcasted_iota(jnp.int32, (128, 128), 0)
    j128 = lax.broadcasted_iota(jnp.int32, (128, 128), 1)
    unit = jnp.where(i128 == j128, 1.0, 0.0).astype(F32)
    a_ref[0:128, 0:128] = s_ref[o:o + 128, o:o + 128]
    a_ref[0:128, 128:256] = unit
    a_ref[128:136, :] = jnp.zeros((8, 256), F32)
    r_ref[...] = jnp.zeros(r_ref.shape, F32)
    t_ref[...] = jnp.zeros(t_ref.shape, F32)

    def body(s, c):
        eight(s, a_ref, r_ref, t_ref)
        return c

    lax.fori_loop(0, 8, body, 0)
    event()
    lax.fori_loop(8, 16, body, 0)
    event()
    s_ref[o:o + 128, o:o + 128] = unit
    block = jnp.dot(a_ref[0:128, 128:256], s_ref[o:o + 128, :], precision=HI, preferred_element_type=F32)
    s_ref[o:o + 128, :] = block
    if o + 128 < n:
        s_ref[o + 128:, o:o + 128] = jnp.zeros((n - o - 128, 128), F32)
        s_ref[o + 128:, :] -= lax.dot_general(
            block[:, o + 128:], block, TN, precision=HI, preferred_element_type=F32
        )


def kernel_sums(
    m_ref, g_ref, v_ref,
    obf_ref, osh_ref, osl_ref, bth_ref, btl_ref, basis_ref,
    bh, bl, vh, vl, part, proj, ph, pl_, pth, ptl,
    gram, gpair, gland, gsum, inv, w, wpair, wland, wsum,
    a_ref, r_ref, t_ref, x1, y1, y2, x2, colsum, cland,
    send_sem, recv_sem,
):
    f, t = lax.axis_index("fsdp"), lax.axis_index("tp")
    z, core = lax.div(f, 2), lax.rem(f, 2)
    x, y = lax.div(t, 4), lax.rem(t, 4)
    rx = Ring(x, lambda i: (f, i * 4 + y))
    ry = Ring(y, lambda i: (f, x * 4 + i))
    rz = Ring(z, lambda i: (i * 2 + core, t))
    partner = (f + 1 - 2 * core, t)
    links = Links(send_sem, recv_sem)

    peers = (rx.right, rx.left, rx.far, ry.right, ry.left, ry.far, rz.right, rz.left, partner)
    barrier = pltpu.get_barrier_semaphore()
    for device in peers:
        pl.semaphore_signal(barrier, inc=1, device_id=device, device_id_type=MESH)
    pl.semaphore_wait(barrier, len(peers))

    rows = m_ref.shape[0]
    rank = v_ref.shape[1]
    half, r1, r2 = rows // 2, rows // 8, rows // 32
    inv_cols = 1.0 / jnp.sqrt(jnp.float32(COLS))

    vh[...], vl[...] = split(v_ref[...])
    first_a = Reduce(links, rx, part, 0, r1, x1)
    first_b = Reduce(links, ry, part, half, r1, y1)
    for d in (2, 1, 3, 0):
        ia = pl.multiple_of(lax.rem(x + d, 4) * r1, r1)
        ib = pl.multiple_of(half + lax.rem(y + d, 4) * r1, r1)
        highs, lows = [], []
        for i in (ia, ib):
            high, low = split(m_ref[pl.ds(i, r1), :] + g_ref[pl.ds(i, r1), :].astype(F32))
            bh[pl.ds(i, r1), :] = high
            bl[pl.ds(i, r1), :] = low
            highs.append(high)
            lows.append(low)
        value = dot3(jnp.concatenate(highs), jnp.concatenate(lows), vh[...], vl[...]) * inv_cols
        part[pl.ds(ia, r1), :] = value[:r1]
        part[pl.ds(ib, r1), :] = value[r1:]
        if d == 2:
            first_a.relay()
            first_b.relay()
        if d == 3:
            first_a.direct()
            first_b.direct()
    first_a.mid()
    first_b.mid()
    base_a = pl.multiple_of(x * r1, r1)
    base_b = pl.multiple_of(half + y * r1, r1)
    second_a = Reduce(links, ry, part, base_a, r2, y2)
    second_b = Reduce(links, rx, part, base_b, r2, x2)
    for one, base, two in ((first_a, base_a, second_a), (first_b, base_b, second_b)):
        h0, h1 = one.finish()
        part[pl.ds(base, r1 // 2), :] = h0
        part[pl.ds(pl.multiple_of(base + r1 // 2, r1 // 2), r1 // 2), :] = h1
        two.relay()
        two.direct()
    second_a.mid()
    second_b.mid()
    third_a = Gather(links, ry, proj, base_a, r2)
    third_b = Gather(links, rx, proj, base_b, r2)
    for two, ring, three in ((second_a, ry, third_a), (second_b, rx, third_b)):
        h0, h1 = two.finish()
        three.half(ring.me, 0)[...] = h0
        three.half(ring.me, 1)[...] = h1
        three.start()
    third_a.mid()
    third_b.mid()
    fourth_a = Gather(links, rx, proj, 0, r1)
    fourth_b = Gather(links, ry, proj, half, r1)
    third_a.finish()
    fourth_a.start()
    third_b.finish()
    fourth_b.start()
    fourth_a.mid()
    fourth_b.mid()
    fourth_a.finish()
    fourth_b.finish()

    step = 256
    def turned(i, c):
        at = pl.multiple_of(i * step, step)
        value = proj[pl.ds(at, step), :]
        ph[pl.ds(at, step), :], pl_[pl.ds(at, step), :] = split(value)
        pth[:, pl.ds(at, step)], ptl[:, pl.ds(at, step)] = split(value.T)
        return c

    lax.fori_loop(0, rows // step, turned, 0)
    tile = 128

    def gram_rows(i, c):
        at = pl.multiple_of(i * tile, tile)
        gram[pl.ds(at, tile), :] = dot3(pth[pl.ds(at, tile), :], ptl[pl.ds(at, tile), :], ph[...], pl_[...])
        return c

    lax.fori_loop(0, rank // tile, gram_rows, 0)
    gs = SumOver8(links, rz, core, partner, gram, gpair, gland, gsum)
    ws = SumOver8(links, rz, core, partner, w, wpair, wland, wsum)
    gs.exchange()
    gs.begin()

    def w_rows(i, c):
        at = pl.multiple_of(i * tile, tile)
        w[pl.ds(at, tile), :] = dot3(pth[pl.ds(at, tile), :], ptl[pl.ds(at, tile), :], bh[...], bl[...])
        return c

    lax.fori_loop(0, rank // tile, w_rows, 0)
    ws.exchange()
    gs.mid()
    gs.turn()
    gs.forward()
    gs.last()
    gs.end()

    rid = lax.broadcasted_iota(jnp.int32, (rank, rank), 0)
    cid = lax.broadcasted_iota(jnp.int32, (rank, rank), 1)
    value = gsum[...]
    diagonal = jnp.where(rid == cid, value, 0.0)
    shift = 0.0001 * jnp.sum(diagonal) / rank
    inv[...] = value + jnp.where(rid == cid, shift, 0.0)
    events = [ws.mid, ws.turn, ws.forward, ws.last, ws.end]

    def event():
        if events:
            events.pop(0)()

    ws.begin()
    for k in range(rank // 128):
        factor_step(k, inv, a_ref, r_ref, t_ref, event)
    while events:
        event()
    xh, xl = split(jnp.where(cid <= rid, inv[...], 0.0))

    wh, wl = split(wsum[...])
    back_t = dot3(xh, xl, wh, wl)
    bth_ref[...], btl_ref[...] = split(back_t)
    back = back_t.T
    total = jnp.sum(back * back, axis=0, keepdims=True)
    basis_ref[...] = back
    for ring, at in ((rx, 0), (ry, 3)):
        colsum[at // 3] = jnp.broadcast_to(total, colsum.shape[1:])
        slots = [links.slot() for _ in range(3)]
        devices = (ring.right, ring.left, ring.far)
        for j, device in enumerate(devices):
            links.send(slots[j], colsum.at[at // 3], cland.at[at + j], device)
        if at == 0:
            ortho = dot3(ph[...], pl_[...], xh, xl, NT)
            obf_ref[...] = ortho.astype(BF16)
        for j, device in enumerate(devices):
            links.landed(slots[j], cland.at[at + j], device)
        for j in range(3):
            total = total + cland[at + j, 0:1, :]
    scales = jnp.sqrt(total / COLS + 1e-06)
    osh_ref[...], osl_ref[...] = split(ortho * (jnp.sqrt(jnp.float32(ROWS) / RANK) / scales))
    basis_ref[...] = basis_ref[...] / scales
    links.drain()


def kernel_outputs(m_ref, g_ref, o_ref, osh_ref, osl_ref, bth_ref, btl_ref, b_ref, mo_ref, bo_ref, u_ref):
    buffer = m_ref[...] + g_ref[...].astype(F32)
    low = jnp.dot(o_ref[...], bth_ref[...], preferred_element_type=F32)
    mo_ref[...] = buffer - 0.05 * low
    u_ref[...] = dot3(osh_ref[...], osl_ref[...], bth_ref[...], btl_ref[...]).astype(BF16)
    bo_ref[...] = b_ref[...]


def shards(momentum, gradient, basis):
    rows, cols = momentum.shape
    rank = basis.shape[1]
    r1, r2 = rows // 8, rows // 32

    def mem(shape, kind=F32):
        return pltpu.VMEM(shape, kind)

    def out(shape, kind=F32):
        return jax.ShapeDtypeStruct(shape, kind)

    whole = pl.BlockSpec(memory_space=pltpu.VMEM)
    n = rank // 8
    obf, osh, osl, bth, btl, basis_out = pl.pallas_call(
        kernel_sums,
        out_shape=(
            out((rows, rank), BF16), out((rows, rank), BF16), out((rows, rank), BF16),
            out((rank, cols), BF16), out((rank, cols), BF16), out((cols, rank)),
        ),
        in_specs=[whole] * 3,
        out_specs=(whole,) * 6,
        scratch_shapes=[
            mem((rows, cols), BF16), mem((rows, cols), BF16), mem((cols, rank), BF16), mem((cols, rank), BF16),
            mem((rows, rank)), mem((rows, rank)),
            mem((rows, rank), BF16), mem((rows, rank), BF16), mem((rank, rows), BF16), mem((rank, rows), BF16),
            mem((rank, rank)), mem((rank // 2, rank)), mem((6, n // 2, rank)), mem((rank, rank)), mem((rank, rank)),
            mem((rank, cols)), mem((rank // 2, cols)), mem((6, n // 2, cols)), mem((rank, cols)),
            mem((136, 256)), mem((8, 256)), mem((136, 8)),
            mem((6, r1 // 2, rank)), mem((6, r1 // 2, rank)), mem((6, r2 // 2, rank)), mem((6, r2 // 2, rank)),
            mem((2, 8, rank)), mem((6, 8, rank)),
            pltpu.SemaphoreType.DMA((76,)), pltpu.SemaphoreType.DMA((76,)),
        ],
        compiler_params=pltpu.CompilerParams(
            collective_id=0, has_side_effects=True, vmem_limit_bytes=60 * 2**20
        ),
        cost_estimate=pl.CostEstimate(flops=10 * 10**9, bytes_accessed=20 * 2**20, transcendentals=0),
    )(momentum, gradient, basis)
    tiles = 4
    tr, tc = rows // tiles, cols // tiles

    def rowed(width):
        return pl.BlockSpec((tr, width), lambda i: (i, 0))

    fixed = pl.BlockSpec((rank, cols), lambda i: (0, 0))
    cut = pl.BlockSpec((tc, rank), lambda i: (i, 0))
    return pl.pallas_call(
        kernel_outputs,
        grid=(tiles,),
        out_shape=(out((rows, cols)), out((cols, rank)), out((rows, cols), BF16)),
        in_specs=[rowed(cols), rowed(cols), rowed(rank), rowed(rank), rowed(rank), fixed, fixed, cut],
        out_specs=(rowed(cols), cut, rowed(cols)),
        compiler_params=pltpu.CompilerParams(vmem_limit_bytes=40 * 2**20),
        cost_estimate=pl.CostEstimate(flops=4 * 10**9, bytes_accessed=18 * 2**20, transcendentals=0),
    )(momentum, gradient, obf, osh, osl, bth, btl, basis_out)


def solution(mesh):
    placed = (P("fsdp", "tp"), P("fsdp", "tp"), P("tp", None))
    return jax.shard_map(
        shards,
        mesh=mesh,
        in_specs=placed,
        out_specs=(P("fsdp", "tp"), P("tp", None), P("fsdp", "tp")),
        check_vma=False,
    )
```

time: 513 us -> 132 us (0.26); the launches traced: 507 us -> 132 us
  waiting for transfers between devices: 219 us -> 0 us
  other arithmetic: 129 us -> 0 us
  Pallas kernels: 0 us -> 122 us
  matrix products: 79.3 us -> 0 us
  blocking collectives: 40.3 us -> 0 us
  between operations: 17.6 us -> 0.67 us
  local copies, waits for them, and re-layouts: 20.7 us -> 9.03 us
    psum x3 -> x0, waiting for transfers between devices: 219 us -> none  [the longest x1 92.6 us: shards(): proj = lax.psum(partial_proj, 'tp')]
    pallas_call x0 -> x2, Pallas kernels: none -> 122 us  [the longest x1 116 us: shards(): pl.pallas_call(kernel_sums, out_shape=(out((rows, rank), BF16), out((rows...]
    another operation x17 -> x0, other arithmetic: 120 us -> none  [the longest x14 78.9 us: factor_of(): return jnp.linalg.cholesky(gram + shift * jnp.eye(RANK, dtype=jnp.float32))]
    dot_general x5 -> x0, matrix products: 59.3 us -> none  [the longest x1 15.4 us: shards(): momentum_out = buffer - 0.05 * jnp.dot(ortho, back.T, precision=high)]
    psum x1 -> x0, blocking collectives: 40.3 us -> none  [shards(): sums = lax.psum(jnp.sum(back * back, axis=0), 'tp')]
    another operation x13 -> x0, matrix products: 20 us -> none  [the longest x7 14 us: shards(): lax.linalg.triangular_solve(lower, proj, left_side=False, lower=True, tra...]
    another operation x34 -> x0, local copies, waits for them, and re-layouts: 15 us -> none
    unnamed x26 -> x16, local copies, waits for them, and re-layouts: 3.26 us -> 9.03 us
  transfers between devices with their start and end apart: 3 -> 0, of which waited for: 3 -> 0; matrix products, arithmetic and copies ran while one was open for 0% -> 0% of each run, Pallas kernels for 0% -> 0%
where the time goes in v2:
time: 132 us
  Pallas kernels  122 us (92%)
  local copies, waits for them, and re-layouts  9.03 us (7%)
    pallas_call x1, Pallas kernels, shards(): pl.pallas_call(kernel_sums, out_shape=(out((rows, rank), BF16), out((rows...  116 us
    unnamed x16, local copies, waits for them, and re-layouts  9.03 us
    pallas_call x1, Pallas kernels, shards(): pl.pallas_call(kernel_outputs, grid=(tiles,), out_shape=(out((rows, cols)...  6.11 us

profile of v2, /device:TPU:0, one launch (start us, length us, event | category | flops | bytes accessed | tf_op | source)
XLA Modules:
  0.0 132.0 jit_solution(5412713965305717075)
XLA Ops:
  0.6 0.0 copy-start
  0.6 116.2 %shard_map.58 = (bf16[1024,512]{1,0:T(8,128)(2,1)}, bf16[1024,512]{1,0:T(8,128)(2,1)}, bf16[1024,512]{1,0:T(8,128)(2,1)}, bf16[512,896]{1,0:T(8,128)(2,1)}, bf16...) custom-call(f32[1024,896]{1,0:T(8,128)} %m_ref.3, bf16[1024,896]{1,0:T(8,128)(2,1)} %g_ref.3, f32[896,512]{1,0:T(8,128)} %v_ref.1), custom_call_target="tpu_custom_call" | custom-call | flops 10000000000 | bytes 20971520 | tf_op jit(solution)/shard_map/pallas_call | solution.py:446
  116.9 0.0 copy-done
  116.9 0.0 copy-start.1
  116.9 1.5 %copy-done.1 = bf16[1024,896]{1,0:T(8,128)(2,1)S(1)} copy-done((bf16[1024,896]{1,0:T(8,128)(2,1)S(1)}, bf16[1024,896]{1,0:T(8,128)(2,1)}, u32[]{:S(2)}) %copy-start.1) | copy-done | bytes 1835032
  118.4 0.0 copy-start.2
  118.4 1.5 %copy-done.2 = f32[896,512]{1,0:T(8,128)S(1)} copy-done((f32[896,512]{1,0:T(8,128)S(1)}, f32[896,512]{1,0:T(8,128)}, u32[]{:S(2)}) %copy-start.2) | copy-done | bytes 1835032
  119.9 0.0 copy-start.3
  119.9 1.2 copy-done.3
  121.1 0.0 copy-start.4
  121.1 1.2 copy-done.4
  122.3 0.0 copy-start.5
  122.3 1.2 copy-done.5
  123.6 0.0 copy-start.6
  123.6 1.2 copy-done.6
  124.7 0.0 copy-start.7
  124.7 1.2 copy-done.7
  125.9 6.1 %shard_map.59 = (f32[1024,896]{1,0:T(8,128)}, f32[896,512]{1,0:T(8,128)}, bf16[1024,896]{1,0:T(8,128)(2,1)}) custom-call(f32[1024,896]{1,0:T(8,128)S(1)} %copy-done, bf16[1024,896]{1,0:T(8,128)(2,1)S(1)} %copy-done.1, bf16[1024,512]{1,0:T(8,128)(2,1)S(1)} %copy-done.3, bf16[1024,512]{1,0:T(8,128)(2,1)S(1)} %copy-done.4, bf16[1024,512]{1,0:T(8,128)(2,1)S(1)} %copy-done.5, ...), custom_call_target="tpu_custom_call" | custom-call | flops 4000000000 | bytes 18874368 | tf_op jit(solution)/shard_map/pallas_call | solution.py:478
Async XLA Ops:
  0.6 116.3 %copy-start = (f32[1024,896]{1,0:T(8,128)S(1)}, f32[1024,896]{1,0:T(8,128)}, u32[]{:S(2)}) copy-start(f32[1024,896]{1,0:T(8,128)} %m_ref.3) | copy-start | bytes 11010052
  116.9 1.5 %copy-start.1 = (bf16[1024,896]{1,0:T(8,128)(2,1)S(1)}, bf16[1024,896]{1,0:T(8,128)(2,1)}, u32[]{:S(2)}) copy-start(bf16[1024,896]{1,0:T(8,128)(2,1)} %g_ref.3) | copy-start | bytes 5505028
  118.4 1.5 %copy-start.2 = (f32[896,512]{1,0:T(8,128)S(1)}, f32[896,512]{1,0:T(8,128)}, u32[]{:S(2)}) copy-start(f32[896,512]{1,0:T(8,128)} %get-tuple-element.14.b_ref) | copy-start | bytes 5505028
  119.9 1.2 copy-start.3
  121.1 1.2 copy-start.4
  122.3 1.2 copy-start.5
  123.6 1.2 copy-start.6
  124.7 1.2 copy-start.7

commit v3 on v0

v3 whole, which is shorter than its diff:
```python
import functools

import jax
import jax.numpy as jnp
from jax import lax
from jax.experimental import pallas as pl
from jax.experimental.pallas import tpu as pltpu
from jax.sharding import PartitionSpec as P

ROWS = 8192
COLS = 14336
RANK = 512
HI = lax.Precision.HIGHEST
F32 = jnp.float32
BF16 = jnp.bfloat16
MESH = pl.DeviceIdType.MESH
NT = (((1,), (1,)), ((), ()))
TN = (((0,), (0,)), ((), ()))
NN = (((1,), (0,)), ((), ()))


def split(v):
    high = v.astype(BF16)
    return high, (v - high.astype(F32)).astype(BF16)


def dot3(ah, al, bh, bl, dims=NN):
    def one(a, b):
        return lax.dot_general(a, b, dims, preferred_element_type=F32)

    return one(ah, bl) + one(al, bh) + one(ah, bh)


class Links:
    def __init__(self, send_sem, recv_sem):
        self.send_sem, self.recv_sem, self.used, self.sent = send_sem, recv_sem, 0, []

    def slot(self):
        self.used += 1
        return self.used - 1

    def copy(self, slot, src, dst, device):
        return pltpu.make_async_remote_copy(
            src_ref=src,
            dst_ref=dst,
            send_sem=self.send_sem.at[slot],
            recv_sem=self.recv_sem.at[slot],
            device_id=device,
            device_id_type=MESH,
        )

    def send(self, slot, src, dst, device):
        c = self.copy(slot, src, dst, device)
        c.start()
        self.sent.append(c)

    def landed(self, slot, dst, device):
        self.copy(slot, dst, dst, device).wait_recv()

    def drain(self):
        for c in self.sent:
            c.wait_send()
        self.sent = []


class Ring:
    def __init__(self, me, at):
        self.me = me
        self.others = [lax.rem(me + o, 4) for o in (2, 1, 3)]
        self.devices = [at(i) for i in self.others]
        self.sources = [lax.rem(me + o, 4) for o in (2, 3, 1)]


def cut(ref, at, n):
    return ref.at[pl.ds(pl.multiple_of(at, n), n), :]


class Reduce:
    def __init__(self, links, ring, ref, base, rows, land):
        self.k, self.g, self.ref, self.base, self.rows, self.land = links, ring, ref, base, rows, land
        self.s = [links.slot() for _ in range(3)]

    def chunk(self, i):
        return cut(self.ref, self.base + i * self.rows, self.rows)

    def send(self, j):
        self.k.send(self.s[j], self.chunk(self.g.others[j]), self.land.at[j], self.g.devices[j])

    def start(self):
        for j in range(3):
            self.send(j)

    def finish(self):
        for j in range(3):
            self.k.landed(self.s[j], self.land.at[j], self.g.devices[j])
        return (self.chunk(self.g.me)[...] + self.land[0]) + (self.land[1] + self.land[2])


class Gather:
    def __init__(self, links, ring, ref, base, rows):
        self.k, self.g, self.ref, self.base, self.rows = links, ring, ref, base, rows
        self.s = [links.slot() for _ in range(3)]

    def chunk(self, i):
        return cut(self.ref, self.base + i * self.rows, self.rows)

    def start(self):
        own = self.chunk(self.g.me)
        for j in range(3):
            self.k.send(self.s[j], own, own, self.g.devices[j])

    def finish(self):
        for j in range(3):
            self.k.landed(self.s[j], self.chunk(self.g.sources[j]), self.g.devices[j])


class SumOver8:
    def __init__(self, links, ring, core, partner, ref, pair, land, total):
        self.k, self.core, self.partner, self.ref, self.pair, self.total = links, core, partner, ref, pair, total
        self.ring = ring
        self.n = ref.shape[0] // 2
        self.rows = self.n // 4
        self.s = [links.slot() for _ in range(5)]
        self.base = core * self.n
        self.other = (1 - core) * self.n
        self.reduce = Reduce(links, ring, ref, self.base, self.rows, land)
        self.gather = Gather(links, ring, total, self.base, self.rows)

    def exchange(self):
        self.k.send(self.s[0], cut(self.ref, self.other, self.n), self.pair, self.partner)

    def begin(self):
        self.k.landed(self.s[0], self.pair, self.partner)
        own = cut(self.ref, self.base, self.n)
        own[...] += self.pair[...]
        self.reduce.start()

    def pass_on(self, j, chunk):
        part = self.gather.chunk(chunk)
        self.k.send(self.s[1 + j], part, part, self.partner)

    def turn(self):
        self.gather.chunk(self.ring.me)[...] = self.reduce.finish()
        self.gather.start()
        self.pass_on(0, self.ring.me)

    def forward(self):
        self.gather.finish()
        for j in range(3):
            self.pass_on(1 + j, self.ring.sources[j])

    def end(self):
        for j, chunk in enumerate([self.ring.me] + self.ring.sources):
            self.k.landed(self.s[1 + j], cut(self.total, self.other + chunk * self.rows, self.rows), self.partner)


def lane(v, j):
    return jnp.take_along_axis(v, jnp.full(v.shape, j, jnp.int32), axis=1)


def row(v, j):
    return jnp.broadcast_to(v[j:j + 1, :], v.shape)


def eight(s, a_ref, r_ref, t_ref):
    sid = lax.broadcasted_iota(jnp.int32, (8, 128), 0)
    o = pl.multiple_of(8 * s, 8)
    on = pl.multiple_of(8 * s + 8, 8)
    p, q = a_ref[pl.ds(o, 8), 0:128], a_ref[pl.ds(o, 8), 128:256]
    n, nx = a_ref[pl.ds(on, 8), 0:128], a_ref[pl.ds(on, 8), 128:256]
    last = r_ref[...]
    t = t_ref[pl.ds(on, 8), :]
    for j in range(8):
        l = jnp.broadcast_to(t[:, j:j + 1], (8, 128))
        n = n - l * row(last[:, 0:128], j)
        nx = nx - l * row(last[:, 128:256], j)
    cb = [lane(p, 8 * s + j) for j in range(8)]
    cn = [lane(n, 8 * s + j) for j in range(8)]
    for j in range(8):
        d = 1.0 / row(cb[j], j)
        cm = jnp.where(sid > j, cb[j], 0.0)
        for k in range(j + 1, 8):
            m = row(cb[k], j) * d
            cb[k] = cb[k] - cm * m
            cn[k] = cn[k] - cn[j] * m
        u, ux = row(p, j) * d, row(q, j) * d
        p, q = p - cm * u, q - cm * ux
        n, nx = n - cn[j] * u, nx - cn[j] * ux
    pivots = cb[0]
    for j in range(1, 8):
        pivots = jnp.where(sid == j, cb[j], pivots)
    scale = lax.rsqrt(pivots)
    p, q = p * scale, q * scale
    rest = jnp.dot(t_ref[0:128, :], last, precision=HI, preferred_element_type=F32)
    rid = lax.broadcasted_iota(jnp.int32, (128, 256), 0)
    a_ref[0:128, :] -= jnp.where(rid >= 8 * s + 16, rest, 0.0)
    a_ref[pl.ds(o, 8), 128:256] = q
    a_ref[pl.ds(on, 8), 0:128] = n
    a_ref[pl.ds(on, 8), 128:256] = nx
    r_ref[:, 0:128] = p
    r_ref[:, 128:256] = q
    t_ref[0:128, :] = p.T


def factor_step(k, s_ref, a_ref, r_ref, t_ref, event):
    n = s_ref.shape[0]
    o = 128 * k
    i128 = lax.broadcasted_iota(jnp.int32, (128, 128), 0)
    j128 = lax.broadcasted_iota(jnp.int32, (128, 128), 1)
    unit = jnp.where(i128 == j128, 1.0, 0.0).astype(F32)
    a_ref[0:128, 0:128] = s_ref[o:o + 128, o:o + 128]
    a_ref[0:128, 128:256] = unit
    a_ref[128:136, :] = jnp.zeros((8, 256), F32)
    r_ref[...] = jnp.zeros(r_ref.shape, F32)
    t_ref[...] = jnp.zeros(t_ref.shape, F32)

    def body(s, c):
        eight(s, a_ref, r_ref, t_ref)
        return c

    for quarter in range(4):
        lax.fori_loop(4 * quarter, 4 * quarter + 4, body, 0)
        event()
    s_ref[o:o + 128, o:o + 128] = unit
    block = jnp.dot(a_ref[0:128, 128:256], s_ref[o:o + 128, :], precision=HI, preferred_element_type=F32)
    s_ref[o:o + 128, :] = block
    if o + 128 < n:
        s_ref[o + 128:, o:o + 128] = jnp.zeros((n - o - 128, 128), F32)
        s_ref[o + 128:, :] -= lax.dot_general(
            block[:, o + 128:], block, TN, precision=HI, preferred_element_type=F32
        )


def full(a, b, dims=NN):
    return lax.dot_general(a, b, dims, precision=HI, preferred_element_type=F32)


def kernel_sums(
    m_hbm, g_hbm, v_hbm,
    oh_hbm, ol_hbm, bth_hbm, btl_hbm, basis_hbm, sc_hbm,
    m_ref, g_ref, v_ref, oh_ref, ol_ref, bth_ref, btl_ref, basis_ref, sc_ref,
    bh, bl, vh, vl, part, proj, ph, pl_, pth, ptl,
    gram0, gpair0, gland0, gsum0, gram1, gpair1, gland1, gsum1, w, wpair, wland, wsum,
    s0, s1, s2, a_ref, r_ref, t_ref, x1, y1, y2, x2, tbuf, tland, colsum, cland,
    in_sem, out_sem, send_sem, recv_sem,
):
    f, t = lax.axis_index("fsdp"), lax.axis_index("tp")
    z, core = lax.div(f, 2), lax.rem(f, 2)
    x, y = lax.div(t, 4), lax.rem(t, 4)
    rows = m_ref.shape[0]
    rank = v_ref.shape[1]
    half, r1, r2 = rows // 2, rows // 8, rows // 32
    wide = rank // 2

    v_in = pltpu.make_async_copy(v_hbm, v_ref, in_sem.at[0])
    v_in.start()
    spans, arrivals = [], []
    for j, d in enumerate((2, 1, 3, 0)):
        pair = (
            pl.multiple_of(lax.rem(x + d, 4) * r1, r1),
            pl.multiple_of(half + lax.rem(y + d, 4) * r1, r1),
        )
        spans.append(pair)
        arrivals.append([])
        for i, at in enumerate(pair):
            for l, (src, dst) in enumerate(((m_hbm, m_ref), (g_hbm, g_ref))):
                c = pltpu.make_async_copy(
                    src.at[pl.ds(at, r1), :], dst.at[pl.ds(at, r1), :], in_sem.at[1 + 4 * j + 2 * i + l]
                )
                c.start()
                arrivals[-1].append(c)

    rx = Ring(x, lambda i: (f, i * 4 + y))
    ry = Ring(y, lambda i: (f, x * 4 + i))
    rz = Ring(z, lambda i: (i * 2 + core, t))
    partner = (f + 1 - 2 * core, t)
    plane = [(f, lax.rem(t + o, 16)) for o in range(1, 16)]
    links = Links(send_sem, recv_sem)
    peers = plane + rz.devices + [partner]
    barrier = pltpu.get_barrier_semaphore()
    for device in peers:
        pl.semaphore_signal(barrier, inc=1, device_id=device, device_id_type=MESH)
    pl.semaphore_wait(barrier, len(peers))

    base_a, base_b = spans[3]
    first, second, third, fourth = [], [], [], []
    for q in range(4):
        pq, fq = part.at[q], proj.at[q]
        first.append((Reduce(links, rx, pq, 0, r1, x1.at[q]), Reduce(links, ry, pq, half, r1, y1.at[q])))
        second.append((Reduce(links, ry, pq, base_a, r2, y2.at[q]), Reduce(links, rx, pq, base_b, r2, x2.at[q])))
        third.append((Gather(links, ry, fq, base_a, r2), Gather(links, rx, fq, base_b, r2)))
        fourth.append((Gather(links, rx, fq, 0, r1), Gather(links, ry, fq, half, r1)))

    inv_cols = 1.0 / jnp.sqrt(jnp.float32(COLS))
    v_in.wait()
    vh[...], vl[...] = split(v_ref[...])
    for h in range(2):
        for j in range(4):
            if h == 0:
                for c in arrivals[j]:
                    c.wait()
                for at in spans[j]:
                    high, low = split(m_ref[pl.ds(at, r1), :] + g_ref[pl.ds(at, r1), :].astype(F32))
                    bh[pl.ds(at, r1), :] = high
                    bl[pl.ds(at, r1), :] = low
            highs = jnp.concatenate([bh[pl.ds(at, r1), :] for at in spans[j]])
            lows = jnp.concatenate([bl[pl.ds(at, r1), :] for at in spans[j]])
            col = slice(h * wide, (h + 1) * wide)
            value = dot3(highs, lows, vh[:, col], vl[:, col]) * inv_cols
            for i in range(2):
                q = 2 * h + i
                for l, at in enumerate(spans[j]):
                    part[q, pl.ds(at, r1), :] = value[l * r1:(l + 1) * r1, i * 128:(i + 1) * 128]
                if j < 3:
                    for one in first[q]:
                        one.send(j)

    for q in range(4):
        for one, two in zip(first[q], second[q]):
            one.chunk(one.g.me)[...] = one.finish()
            two.start()
    for q in range(4):
        for two, three in zip(second[q], third[q]):
            three.chunk(three.g.me)[...] = two.finish()
            three.start()
    for q in range(4):
        for three, four in zip(third[q], fourth[q]):
            three.finish()
            four.start()

    g0 = SumOver8(links, rz, core, partner, gram0, gpair0, gland0, gsum0)
    g1 = SumOver8(links, rz, core, partner, gram1, gpair1, gland1, gsum1)
    ws = [
        SumOver8(links, rz, core, partner, w.at[h], wpair.at[h], wland.at[h], wsum.at[h]) for h in range(2)
    ]

    def turned(h):
        step = 256
        for q in (2 * h, 2 * h + 1):
            for four in fourth[q]:
                four.finish()

            def body(i, c):
                at = pl.multiple_of(i * step, step)
                value = proj[q, pl.ds(at, step), :]
                col = slice(q * 128, (q + 1) * 128)
                ph[pl.ds(at, step), col], pl_[pl.ds(at, step), col] = split(value)
                pth[col, pl.ds(at, step)], ptl[col, pl.ds(at, step)] = split(value.T)
                return c

            lax.fori_loop(0, rows // step, body, 0)

    def products(h):
        col = slice(h * wide, (h + 1) * wide)
        w[h] = dot3(pth[col, :], ptl[col, :], bh[...], bl[...])

    turned(0)
    gram0[...] = dot3(pth[:wide, :], ptl[:wide, :], ph[:, :wide], pl_[:, :wide])
    g0.exchange()
    products(0)
    g0.begin()
    ws[0].exchange()
    turned(1)
    gram1[...] = dot3(pth[wide:, :], ptl[wide:, :], ph[...], pl_[...])
    g1.exchange()
    squares = jnp.zeros((8, 128), F32)
    for q in range(4):
        value = proj[q]
        squares = squares + jnp.sum((value * value).reshape(rows // 8, 8, 128), axis=0)
    tbuf[0] = squares
    tslots = [links.slot() for _ in range(4)]
    links.send(tslots[0], tbuf.at[0], tland.at[4], partner)
    g1.begin()
    links.landed(tslots[0], tland.at[4], partner)
    tland[z] = tbuf[0] + tland[4]
    for j in range(3):
        links.send(tslots[1 + j], tland.at[z], tland.at[z], rz.devices[j])
    g0.turn()
    products(1)
    ws[1].exchange()
    ws[0].begin()
    for j in range(3):
        links.landed(tslots[1 + j], tland.at[rz.sources[j]], rz.devices[j])
    shift = 0.0001 * jnp.sum(((tland[0] + tland[1]) + tland[2]) + tland[3]) / rank
    g0.forward()
    g0.end()

    rid = lax.broadcasted_iota(jnp.int32, (wide, wide), 0)
    cid = lax.broadcasted_iota(jnp.int32, (wide, wide), 1)
    diagonal = jnp.where(rid == cid, shift, 0.0)
    events = [None, g1.turn, ws[1].begin, None, ws[0].turn, g1.forward, g1.end, None,
              ws[1].turn, None, ws[0].forward, None, None, None, ws[1].forward, None]

    def event():
        e = events.pop(0)
        if e is not None:
            e()

    s0[...] = gsum0[...] + diagonal
    for k in range(wide // 128):
        factor_step(k, s0, a_ref, r_ref, t_ref, event)
    inv0 = jnp.where(cid <= rid, s0[...], 0.0)
    s0[...] = inv0
    low = full(gsum1[:, :wide], inv0, NT)
    s1[...] = gsum1[:, wide:] + diagonal - full(low, low, NT)
    s2[...] = full(low, inv0)
    for k in range(wide // 128):
        factor_step(k, s1, a_ref, r_ref, t_ref, event)
    inv1 = jnp.where(cid <= rid, s1[...], 0.0)
    x0h, x0l = split(s0[...])
    x1h, x1l = split(inv1)
    xch, xcl = split(-full(inv1, s2[...]))
    ws[0].end()
    ws[1].end()

    w0h, w0l = split(wsum[0])
    w1h, w1l = split(wsum[1])
    sums = []
    for h in range(2):
        col = slice(h * wide, (h + 1) * wide)
        if h == 0:
            back_t = dot3(x0h, x0l, w0h, w0l)
        else:
            back_t = dot3(xch, xcl, w0h, w0l) + dot3(x1h, x1l, w1h, w1l)
        bth_ref[col, :], btl_ref[col, :] = split(back_t)
        back = back_t.T
        basis_ref[:, col] = back
        sums.append(jnp.sum(back * back, axis=0, keepdims=True))
    total = jnp.concatenate(sums, axis=1)
    colsum[...] = jnp.broadcast_to(total, colsum.shape)
    cslots = [links.slot() for _ in plane]
    for o, device in enumerate(plane):
        links.send(cslots[o], colsum, cland.at[o], device)
    outs = [(bth_ref, bth_hbm), (btl_ref, btl_hbm), (basis_ref, basis_hbm)]
    copies = []

    def store(src, dst):
        copies.append(pltpu.make_async_copy(src, dst, out_sem.at[len(copies)]))
        copies[-1].start()

    for src, dst in outs:
        store(src, dst)
    oh_ref[:, :wide], ol_ref[:, :wide] = split(dot3(ph[:, :wide], pl_[:, :wide], x0h, x0l, NT))
    oh_ref[:, wide:], ol_ref[:, wide:] = split(
        dot3(ph[:, :wide], pl_[:, :wide], xch, xcl, NT) + dot3(ph[:, wide:], pl_[:, wide:], x1h, x1l, NT)
    )
    store(oh_ref, oh_hbm)
    store(ol_ref, ol_hbm)
    links.drain()
    for o, device in enumerate(plane):
        links.landed(cslots[o], cland.at[o], device)
        total = total + cland[o, 0:1, :]
    sc_ref[...] = jnp.broadcast_to(1.0 / jnp.sqrt(total / COLS + 1e-06), sc_ref.shape)
    store(sc_ref, sc_hbm)
    for c in copies:
        c.wait()


def kernel_outputs(m_ref, g_ref, oh_ref, ol_ref, bth_ref, btl_ref, b_ref, sc_ref, mo_ref, bo_ref, u_ref):
    buffer = m_ref[...] + g_ref[...].astype(F32)
    low = jnp.dot(oh_ref[...], bth_ref[...], preferred_element_type=F32)
    mo_ref[...] = buffer - 0.05 * low
    scale = sc_ref[0:1, :]
    ortho = oh_ref[...].astype(F32) + ol_ref[...].astype(F32)
    high, rest = split(ortho * (scale * jnp.sqrt(jnp.float32(ROWS) / RANK)))
    u_ref[...] = dot3(high, rest, bth_ref[...], btl_ref[...]).astype(BF16)
    bo_ref[...] = b_ref[...] * scale


def sums_call(momentum, gradient, basis):
    rows, cols = momentum.shape
    rank = basis.shape[1]
    r1, r2, wide = rows // 8, rows // 32, rank // 2

    def mem(shape, kind=F32):
        return pltpu.VMEM(shape, kind)

    def out(shape, kind=F32):
        return jax.ShapeDtypeStruct(shape, kind)

    outs = (
        ((rows, rank), BF16), ((rows, rank), BF16), ((rank, cols), BF16), ((rank, cols), BF16),
        ((cols, rank), F32), ((8, rank), F32),
    )
    n = wide // 8
    anywhere = pl.BlockSpec(memory_space=pl.ANY)
    return pl.pallas_call(
        kernel_sums,
        out_shape=tuple(out(*o) for o in outs),
        in_specs=[anywhere] * 3,
        out_specs=(anywhere,) * 6,
        scratch_shapes=[
            mem((rows, cols)), mem((rows, cols), BF16), mem((cols, rank)),
            *(mem(*o) for o in outs),
            mem((rows, cols), BF16), mem((rows, cols), BF16), mem((cols, rank), BF16), mem((cols, rank), BF16),
            mem((4, rows, 128)), mem((4, rows, 128)),
            mem((rows, rank), BF16), mem((rows, rank), BF16), mem((rank, rows), BF16), mem((rank, rows), BF16),
            mem((wide, wide)), mem((wide // 2, wide)), mem((3, n, wide)), mem((wide, wide)),
            mem((wide, rank)), mem((wide // 2, rank)), mem((3, n, rank)), mem((wide, rank)),
            mem((2, wide, cols)), mem((2, wide // 2, cols)), mem((2, 3, n, cols)), mem((2, wide, cols)),
            mem((wide, wide)), mem((wide, wide)), mem((wide, wide)),
            mem((136, 256)), mem((8, 256)), mem((136, 8)),
            mem((4, 3, r1, 128)), mem((4, 3, r1, 128)), mem((4, 3, r2, 128)), mem((4, 3, r2, 128)),
            mem((1, 8, 128)), mem((5, 8, 128)), mem((8, rank)), mem((15, 8, rank)),
            pltpu.SemaphoreType.DMA((17,)), pltpu.SemaphoreType.DMA((6,)),
            pltpu.SemaphoreType.DMA((160,)), pltpu.SemaphoreType.DMA((160,)),
        ],
        compiler_params=pltpu.CompilerParams(
            collective_id=0, has_side_effects=True, vmem_limit_bytes=62 * 2**20
        ),
        cost_estimate=pl.CostEstimate(flops=10 * 10**9, bytes_accessed=20 * 2**20, transcendentals=0),
    )(momentum, gradient, basis)


def shards(momentum, gradient, basis):
    rows, cols = momentum.shape
    rank = basis.shape[1]

    def out(shape, kind=F32):
        return jax.ShapeDtypeStruct(shape, kind)

    oh, ol, bth, btl, back, scale = sums_call(momentum, gradient, basis)
    tiles = 4
    tr, tc = rows // tiles, cols // tiles

    def rowed(width):
        return pl.BlockSpec((tr, width), lambda i: (i, 0))

    fixed = pl.BlockSpec((rank, cols), lambda i: (0, 0))
    cut_cols = pl.BlockSpec((tc, rank), lambda i: (i, 0))
    small = pl.BlockSpec((8, rank), lambda i: (0, 0))
    return pl.pallas_call(
        kernel_outputs,
        grid=(tiles,),
        out_shape=(out((rows, cols)), out((cols, rank)), out((rows, cols), BF16)),
        in_specs=[rowed(cols), rowed(cols), rowed(rank), rowed(rank), fixed, fixed, cut_cols, small],
        out_specs=(rowed(cols), cut_cols, rowed(cols)),
        compiler_params=pltpu.CompilerParams(vmem_limit_bytes=62 * 2**20),
        cost_estimate=pl.CostEstimate(flops=4 * 10**9, bytes_accessed=18 * 2**20, transcendentals=0),
    )(momentum, gradient, oh, ol, bth, btl, back, scale)


def solution(mesh):
    placed = (P("fsdp", "tp"), P("fsdp", "tp"), P("tp", None))
    return jax.shard_map(
        shards,
        mesh=mesh,
        in_specs=placed,
        out_specs=(P("fsdp", "tp"), P("tp", None), P("fsdp", "tp")),
        check_vma=False,
    )
```

time: 513 us -> 101 us (0.20); the launches traced: 507 us -> 100 us
  waiting for transfers between devices: 219 us -> 0 us
  other arithmetic: 129 us -> 0 us
  Pallas kernels: 0 us -> 99.7 us
  matrix products: 79.3 us -> 0 us
  blocking collectives: 40.3 us -> 0 us
  local copies, waits for them, and re-layouts: 20.7 us -> 0 us
  between operations: 17.6 us -> 0.64 us
    psum x3 -> x0, waiting for transfers between devices: 219 us -> none  [the longest x1 92.6 us: shards(): proj = lax.psum(partial_proj, 'tp')]
    another operation x17 -> x0, other arithmetic: 120 us -> none  [the longest x14 78.9 us: factor_of(): return jnp.linalg.cholesky(gram + shift * jnp.eye(RANK, dtype=jnp.float32))]
    pallas_call x0 -> x2, Pallas kernels: none -> 99.7 us  [the longest x1 90.2 us: sums_call(): pl.pallas_call(kernel_sums, out_shape=tuple((out(*o) for o in outs)), in_...]
    dot_general x5 -> x0, matrix products: 59.3 us -> none  [the longest x1 15.4 us: shards(): momentum_out = buffer - 0.05 * jnp.dot(ortho, back.T, precision=high)]
    psum x1 -> x0, blocking collectives: 40.3 us -> none  [shards(): sums = lax.psum(jnp.sum(back * back, axis=0), 'tp')]
    another operation x13 -> x0, matrix products: 20 us -> none  [the longest x7 14 us: shards(): lax.linalg.triangular_solve(lower, proj, left_side=False, lower=True, tra...]
    another operation x34 -> x0, local copies, waits for them, and re-layouts: 15 us -> none
  transfers between devices with their start and end apart: 3 -> 0, of which waited for: 3 -> 0; matrix products, arithmetic and copies ran while one was open for 0% -> 0% of each run, Pallas kernels for 0% -> 0%
where the time goes in v3:
time: 101 us; the launch traced here: 100 us
  Pallas kernels  99.7 us (99%)
    pallas_call x1, Pallas kernels, sums_call(): pl.pallas_call(kernel_sums, out_shape=tuple((out(*o) for o in outs)), in_...  90.2 us
    pallas_call x1, Pallas kernels, shards(): pl.pallas_call(kernel_outputs, grid=(tiles,), out_shape=(out((rows, cols)...  9.55 us

profile of v3, /device:TPU:0, one launch (start us, length us, event | category | flops | bytes accessed | tf_op | source)
XLA Modules:
  0.0 100.4 jit_solution(9152378748453975191)
XLA Ops:
  0.6 90.2 %shard_map.58 = (bf16[1024,512]{1,0:T(8,128)(2,1)}, bf16[1024,512]{1,0:T(8,128)(2,1)}, bf16[512,896]{1,0:T(8,128)(2,1)}, bf16[512,896]{1,0:T(8,128)(2,1)}, f32[896,512]{1,0:T(8,128)}, /*index=5*/f32[8,512]{1,0:T(8,128)}) custom-call(f32[1024,896]{1,0:T(8,128)} %m_ref.1, bf16[1024,896]{1,0:T(8,128)(2,1)} %g_ref.1, f32[896,512]{1,0:T(8,128)} %v_hbm.1), custom_call_target="tpu_custom_call" | custom-call | flops 10000000000 | bytes 20971520 | tf_op jit(solution)/shard_map/pallas_call | solution.py:487
  90.8 9.6 %shard_map.59 = (f32[1024,896]{1,0:T(8,128)}, f32[896,512]{1,0:T(8,128)}, bf16[1024,896]{1,0:T(8,128)(2,1)}) custom-call(f32[1024,896]{1,0:T(8,128)} %m_ref.1, bf16[1024,896]{1,0:T(8,128)(2,1)} %g_ref.1, bf16[1024,512]{1,0:T(8,128)(2,1)} %get-tuple-element.9.oh_ref, bf16[1024,512]{1,0:T(8,128)(2,1)} %get-tuple-element.10.ol_ref, ...), custom_call_target="tpu_custom_call" | custom-call | flops 4000000000 | bytes 18874368 | tf_op jit(solution)/shard_map/pallas_call | solution.py:532

commit v4 on v3

--- a/solution.py
+++ b/solution.py
@@ -114,8 +114,71 @@
             self.k.landed(self.s[j], self.chunk(self.g.sources[j]), self.g.devices[j])
 
 
+class RelayReduce(Reduce):
+    def __init__(self, links, ring, ref, base, rows, land):
+        self.k, self.g, self.ref, self.base, self.rows, self.land = links, ring, ref, base, rows // 2, land
+        self.s = [links.slot() for _ in range(6)]
+
+    def half(self, i, h):
+        return cut(self.ref, self.base + (2 * i + h) * self.rows, self.rows)
+
+    def relay(self):
+        for d in range(2):
+            self.k.send(self.s[d], self.half(self.g.others[0], d), self.land.at[d], self.g.devices[1 + d])
+
+    def direct(self):
+        for d in range(2):
+            part = self.half(self.g.others[1 + d], 1 - d)
+            self.k.send(self.s[2 + d], part, self.land.at[2 + d], self.g.devices[1 + d])
+
+    def start(self):
+        self.relay()
+        self.direct()
+
+    def mid(self):
+        for d in range(2):
+            self.k.landed(self.s[d], self.land.at[d], self.g.devices[1 + d])
+            part = self.half(self.g.others[1 + d], d)
+            part[...] += self.land[d]
+            self.k.send(self.s[4 + d], part, self.land.at[4 + d], self.g.devices[1 + d])
+
+    def finish(self):
+        for j in range(2, 6):
+            self.k.landed(self.s[j], self.land.at[j], self.g.devices[1])
+        own = [self.half(self.g.me, d)[...] + self.land[4 + d] + self.land[3 - d] for d in range(2)]
+        return jnp.concatenate(own)
+
+    def chunk(self, i):
+        return cut(self.ref, self.base + i * 2 * self.rows, 2 * self.rows)
+
+
+class RelayGather(Gather):
+    def __init__(self, links, ring, ref, base, rows):
+        super().__init__(links, ring, ref, base, rows)
+        self.s.append(links.slot())
+
+    def half(self, i, h):
+        n = self.rows // 2
+        return cut(self.ref, self.base + i * self.rows + h * n, n)
+
+    def start(self):
+        own = self.chunk(self.g.me)
+        for d in range(2):
+            self.k.send(self.s[d], own, own, self.g.devices[1 + d])
+
+    def mid(self):
+        for d in range(2):
+            self.k.landed(self.s[d], self.chunk(self.g.sources[1 + d]), self.g.devices[1 + d])
+            part = self.half(self.g.sources[1 + d], d)
+            self.k.send(self.s[2 + d], part, part, self.g.devices[1 + d])
+
+    def finish(self):
+        for d in range(2):
+            self.k.landed(self.s[2 + d], self.half(self.g.others[0], d), self.g.devices[1 + d])
+
+
 class SumOver8:
-    def __init__(self, links, ring, core, partner, ref, pair, land, total):
+    def __init__(self, links, ring, core, partner, ref, pair, land, total, relay=False):
         self.k, self.core, self.partner, self.ref, self.pair, self.total = links, core, partner, ref, pair, total
         self.ring = ring
         self.n = ref.shape[0] // 2
@@ -123,8 +186,9 @@
         self.s = [links.slot() for _ in range(5)]
         self.base = core * self.n
         self.other = (1 - core) * self.n
-        self.reduce = Reduce(links, ring, ref, self.base, self.rows, land)
-        self.gather = Gather(links, ring, total, self.base, self.rows)
+        self.relay = relay
+        self.reduce = (RelayReduce if relay else Reduce)(links, ring, ref, self.base, self.rows, land)
+        self.gather = (RelayGather if relay else Gather)(links, ring, total, self.base, self.rows)
 
     def exchange(self):
         self.k.send(self.s[0], cut(self.ref, self.other, self.n), self.pair, self.partner)
@@ -144,10 +208,20 @@
         self.gather.start()
         self.pass_on(0, self.ring.me)
 
+    def mid(self):
+        self.reduce.mid()
+
     def forward(self):
+        if self.relay:
+            self.gather.mid()
+        else:
+            self.last()
+        for j in (1, 2):
+            self.pass_on(1 + j, self.ring.sources[j])
+
+    def last(self):
         self.gather.finish()
-        for j in range(3):
-            self.pass_on(1 + j, self.ring.sources[j])
+        self.pass_on(1, self.ring.sources[0])
 
     def end(self):
         for j, chunk in enumerate([self.ring.me] + self.ring.sources):
@@ -160,6 +234,12 @@
 
 def row(v, j):
     return jnp.broadcast_to(v[j:j + 1, :], v.shape)
+
+
+def tree(terms):
+    while len(terms) > 1:
+        terms = [terms[i] + terms[i + 1] for i in range(0, len(terms), 2)]
+    return terms[0]
 
 
 def eight(s, a_ref, r_ref, t_ref):
@@ -170,25 +250,30 @@
     n, nx = a_ref[pl.ds(on, 8), 0:128], a_ref[pl.ds(on, 8), 128:256]
     last = r_ref[...]
     t = t_ref[pl.ds(on, 8), :]
+    terms, termsx = [], []
     for j in range(8):
         l = jnp.broadcast_to(t[:, j:j + 1], (8, 128))
-        n = n - l * row(last[:, 0:128], j)
-        nx = nx - l * row(last[:, 128:256], j)
+        terms.append(l * row(last[:, 0:128], j))
+        termsx.append(l * row(last[:, 128:256], j))
+    n, nx = n - tree(terms), nx - tree(termsx)
     cb = [lane(p, 8 * s + j) for j in range(8)]
     cn = [lane(n, 8 * s + j) for j in range(8)]
+    pivot = row(cb[0], 0)
+    pivots = pivot
     for j in range(8):
-        d = 1.0 / row(cb[j], j)
+        d = 1.0 / pivot
         cm = jnp.where(sid > j, cb[j], 0.0)
+        if j < 7:
+            e = row(cb[j], j + 1)
+            pivot = row(cb[j + 1], j + 1) - (e * e) * d
+            pivots = jnp.where(sid > j, pivot, pivots)
         for k in range(j + 1, 8):
-            m = row(cb[k], j) * d
-            cb[k] = cb[k] - cm * m
-            cn[k] = cn[k] - cn[j] * m
+            m = row(cb[k], j)
+            cb[k] = cb[k] - (cm * m) * d
+            cn[k] = cn[k] - cn[j] * (m * d)
         u, ux = row(p, j) * d, row(q, j) * d
         p, q = p - cm * u, q - cm * ux
         n, nx = n - cn[j] * u, nx - cn[j] * ux
-    pivots = cb[0]
-    for j in range(1, 8):
-        pivots = jnp.where(sid == j, cb[j], pivots)
     scale = lax.rsqrt(pivots)
     p, q = p * scale, q * scale
     rest = jnp.dot(t_ref[0:128, :], last, precision=HI, preferred_element_type=F32)
@@ -237,7 +322,7 @@
 
 def kernel_sums(
     m_hbm, g_hbm, v_hbm,
-    oh_hbm, ol_hbm, bth_hbm, btl_hbm, basis_hbm, sc_hbm,
+    oh_hbm, ol_hbm, bth_hbm, btl_hbm, basis_hbm, sc_hbm, mo_hbm,
     m_ref, g_ref, v_ref, oh_ref, ol_ref, bth_ref, btl_ref, basis_ref, sc_ref,
     bh, bl, vh, vl, part, proj, ph, pl_, pth, ptl,
     gram0, gpair0, gland0, gsum0, gram1, gpair1, gland1, gsum1, w, wpair, wland, wsum,
@@ -251,6 +336,17 @@
     rank = v_ref.shape[1]
     half, r1, r2 = rows // 2, rows // 8, rows // 32
     wide = rank // 2
+
+    rx = Ring(x, lambda i: (f, i * 4 + y))
+    ry = Ring(y, lambda i: (f, x * 4 + i))
+    rz = Ring(z, lambda i: (i * 2 + core, t))
+    partner = (f + 1 - 2 * core, t)
+    plane = [(f, lax.rem(t + o, 16)) for o in range(1, 16)]
+    links = Links(send_sem, recv_sem)
+    peers = plane + rz.devices + [partner]
+    barrier = pltpu.get_barrier_semaphore()
+    for device in peers:
+        pl.semaphore_signal(barrier, inc=1, device_id=device, device_id_type=MESH)
 
     v_in = pltpu.make_async_copy(v_hbm, v_ref, in_sem.at[0])
     v_in.start()
@@ -270,26 +366,18 @@
                 c.start()
                 arrivals[-1].append(c)
 
-    rx = Ring(x, lambda i: (f, i * 4 + y))
-    ry = Ring(y, lambda i: (f, x * 4 + i))
-    rz = Ring(z, lambda i: (i * 2 + core, t))
-    partner = (f + 1 - 2 * core, t)
-    plane = [(f, lax.rem(t + o, 16)) for o in range(1, 16)]
-    links = Links(send_sem, recv_sem)
-    peers = plane + rz.devices + [partner]
-    barrier = pltpu.get_barrier_semaphore()
-    for device in peers:
-        pl.semaphore_signal(barrier, inc=1, device_id=device, device_id_type=MESH)
-    pl.semaphore_wait(barrier, len(peers))
-
     base_a, base_b = spans[3]
     first, second, third, fourth = [], [], [], []
     for q in range(4):
         pq, fq = part.at[q], proj.at[q]
-        first.append((Reduce(links, rx, pq, 0, r1, x1.at[q]), Reduce(links, ry, pq, half, r1, y1.at[q])))
+        first.append((RelayReduce(links, rx, pq, 0, r1, x1.at[q]), RelayReduce(links, ry, pq, half, r1, y1.at[q])))
         second.append((Reduce(links, ry, pq, base_a, r2, y2.at[q]), Reduce(links, rx, pq, base_b, r2, x2.at[q])))
         third.append((Gather(links, ry, fq, base_a, r2), Gather(links, rx, fq, base_b, r2)))
-        fourth.append((Gather(links, rx, fq, 0, r1), Gather(links, ry, fq, half, r1)))
+        fourth.append((RelayGather(links, rx, fq, 0, r1), RelayGather(links, ry, fq, half, r1)))
+
+    def add(q):
+        for one in first[q]:
+            one.mid()
 
     inv_cols = 1.0 / jnp.sqrt(jnp.float32(COLS))
     v_in.wait()
@@ -311,85 +399,104 @@
                 q = 2 * h + i
                 for l, at in enumerate(spans[j]):
                     part[q, pl.ds(at, r1), :] = value[l * r1:(l + 1) * r1, i * 128:(i + 1) * 128]
-                if j < 3:
-                    for one in first[q]:
-                        one.send(j)
-
-    for q in range(4):
+                if h == 0 and j == 0 and i == 0:
+                    pl.semaphore_wait(barrier, len(peers))
+                for one in first[q]:
+                    if j == 0:
+                        one.relay()
+                    if j == 2:
+                        one.direct()
+            if h == 1 and j == 2:
+                add(0)
+                add(1)
+
+    def step1(q):
         for one, two in zip(first[q], second[q]):
             one.chunk(one.g.me)[...] = one.finish()
             two.start()
-    for q in range(4):
+
+    def step2(q):
         for two, three in zip(second[q], third[q]):
             three.chunk(three.g.me)[...] = two.finish()
             three.start()
-    for q in range(4):
+
+    def step3(q):
         for three, four in zip(third[q], fourth[q]):
             three.finish()
             four.start()
 
+    def step4(q):
+        for four in fourth[q]:
+            four.mid()
+
+    add(2)
+    add(3)
+    for stage in (step1, step2, step3, step4):
+        for q in range(4):
+            stage(q)
+
     g0 = SumOver8(links, rz, core, partner, gram0, gpair0, gland0, gsum0)
     g1 = SumOver8(links, rz, core, partner, gram1, gpair1, gland1, gsum1)
     ws = [
-        SumOver8(links, rz, core, partner, w.at[h], wpair.at[h], wland.at[h], wsum.at[h]) for h in range(2)
+        SumOver8(links, rz, core, partner, w.at[h], wpair.at[h], wland.at[h], wsum.at[h], True) for h in range(2)
     ]
 
-    def turned(h):
+    def turned(q):
         step = 256
-        for q in (2 * h, 2 * h + 1):
-            for four in fourth[q]:
-                four.finish()
-
-            def body(i, c):
-                at = pl.multiple_of(i * step, step)
-                value = proj[q, pl.ds(at, step), :]
-                col = slice(q * 128, (q + 1) * 128)
-                ph[pl.ds(at, step), col], pl_[pl.ds(at, step), col] = split(value)
-                pth[col, pl.ds(at, step)], ptl[col, pl.ds(at, step)] = split(value.T)
-                return c
-
-            lax.fori_loop(0, rows // step, body, 0)
-
-    def products(h):
-        col = slice(h * wide, (h + 1) * wide)
-        w[h] = dot3(pth[col, :], ptl[col, :], bh[...], bl[...])
-
-    turned(0)
+        for four in fourth[q]:
+            four.finish()
+        col = slice(q * 128, (q + 1) * 128)
+
+        def body(i, c):
+            at = pl.multiple_of(i * step, step)
+            value = proj[q, pl.ds(at, step), :]
+            ph[pl.ds(at, step), col], pl_[pl.ds(at, step), col] = split(value)
+            pth[col, pl.ds(at, step)], ptl[col, pl.ds(at, step)] = split(value.T)
+            return c + jnp.sum((value * value).reshape(step // 8, 8, 128), axis=0)
+
+        return lax.fori_loop(0, rows // step, body, jnp.zeros((8, 128), F32))
+
+    def products(h, i):
+        at = h * wide + i * 128
+        col = slice(at, at + 128)
+        w[h, i * 128:(i + 1) * 128, :] = dot3(pth[col, :], ptl[col, :], bh[...], bl[...])
+
+    squares = turned(0)
+    squares = squares + turned(1)
     gram0[...] = dot3(pth[:wide, :], ptl[:wide, :], ph[:, :wide], pl_[:, :wide])
     g0.exchange()
-    products(0)
+    squares = squares + turned(2)
     g0.begin()
-    ws[0].exchange()
-    turned(1)
-    gram1[...] = dot3(pth[wide:, :], ptl[wide:, :], ph[...], pl_[...])
-    g1.exchange()
-    squares = jnp.zeros((8, 128), F32)
-    for q in range(4):
-        value = proj[q]
-        squares = squares + jnp.sum((value * value).reshape(rows // 8, 8, 128), axis=0)
+    squares = squares + turned(3)
     tbuf[0] = squares
     tslots = [links.slot() for _ in range(4)]
     links.send(tslots[0], tbuf.at[0], tland.at[4], partner)
-    g1.begin()
+    gram1[...] = dot3(pth[wide:, :], ptl[wide:, :], ph[...], pl_[...])
+    g1.exchange()
     links.landed(tslots[0], tland.at[4], partner)
     tland[z] = tbuf[0] + tland[4]
     for j in range(3):
         links.send(tslots[1 + j], tland.at[z], tland.at[z], rz.devices[j])
     g0.turn()
-    products(1)
+    products(0, 0)
+    g1.begin()
+    products(0, 1)
+    ws[0].exchange()
+    products(1, 0)
+    ws[0].begin()
+    products(1, 1)
     ws[1].exchange()
-    ws[0].begin()
+    g0.forward()
     for j in range(3):
         links.landed(tslots[1 + j], tland.at[rz.sources[j]], rz.devices[j])
     shift = 0.0001 * jnp.sum(((tland[0] + tland[1]) + tland[2]) + tland[3]) / rank
-    g0.forward()
     g0.end()
 
     rid = lax.broadcasted_iota(jnp.int32, (wide, wide), 0)
     cid = lax.broadcasted_iota(jnp.int32, (wide, wide), 1)
     diagonal = jnp.where(rid == cid, shift, 0.0)
-    events = [None, g1.turn, ws[1].begin, None, ws[0].turn, g1.forward, g1.end, None,
-              ws[1].turn, None, ws[0].forward, None, None, None, ws[1].forward, None]
+    events = [g1.turn, ws[0].mid, ws[1].begin, None, g1.forward, ws[0].turn, g1.end, ws[1].mid,
+              ws[0].forward, ws[1].turn, None, ws[0].last, None, ws[1].forward, None, None]
 
     def event():
         e = events.pop(0)
@@ -410,6 +517,7 @@
     x0h, x0l = split(s0[...])
     x1h, x1l = split(inv1)
     xch, xcl = split(-full(inv1, s2[...]))
+    ws[1].last()
     ws[0].end()
     ws[1].end()
 
@@ -446,6 +554,11 @@
     )
     store(oh_ref, oh_hbm)
     store(ol_ref, ol_hbm)
+    for i in range(4):
+        at = slice(i * rows // 4, (i + 1) * rows // 4)
+        low = jnp.dot(oh_ref[at, :], bth_ref[...], preferred_element_type=F32)
+        m_ref[at, :] = m_ref[at, :] + g_ref[at, :].astype(F32) - 0.05 * low
+        store(m_ref.at[at, :], mo_hbm.at[at, :])
     links.drain()
     for o, device in enumerate(plane):
         links.landed(cslots[o], cland.at[o], device)
@@ -456,13 +569,11 @@
         c.wait()
 
 
-def kernel_outputs(m_ref, g_ref, oh_ref, ol_ref, bth_ref, btl_ref, b_ref, sc_ref, mo_ref, bo_ref, u_ref):
-    buffer = m_ref[...] + g_ref[...].astype(F32)
-    low = jnp.dot(oh_ref[...], bth_ref[...], preferred_element_type=F32)
-    mo_ref[...] = buffer - 0.05 * low
+def kernel_outputs(mi_ref, oh_ref, ol_ref, bth_ref, btl_ref, b_ref, sc_ref, mo_ref, bo_ref, u_ref):
     scale = sc_ref[0:1, :]
     ortho = oh_ref[...].astype(F32) + ol_ref[...].astype(F32)
     high, rest = split(ortho * (scale * jnp.sqrt(jnp.float32(ROWS) / RANK)))
+    mo_ref[...] = mi_ref[...]
     u_ref[...] = dot3(high, rest, bth_ref[...], btl_ref[...]).astype(BF16)
     bo_ref[...] = b_ref[...] * scale
 
@@ -482,13 +593,14 @@
         ((rows, rank), BF16), ((rows, rank), BF16), ((rank, cols), BF16), ((rank, cols), BF16),
         ((cols, rank), F32), ((8, rank), F32),
     )
+    result = out((rows, cols))
     n = wide // 8
     anywhere = pl.BlockSpec(memory_space=pl.ANY)
     return pl.pallas_call(
         kernel_sums,
-        out_shape=tuple(out(*o) for o in outs),
+        out_shape=tuple(out(*o) for o in outs) + (result,),
         in_specs=[anywhere] * 3,
-        out_specs=(anywhere,) * 6,
+        out_specs=(anywhere,) * 7,
         scratch_shapes=[
             mem((rows, cols)), mem((rows, cols), BF16), mem((cols, rank)),
             *(mem(*o) for o in outs),
@@ -497,13 +609,13 @@
             mem((rows, rank), BF16), mem((rows, rank), BF16), mem((rank, rows), BF16), mem((rank, rows), BF16),
             mem((wide, wide)), mem((wide // 2, wide)), mem((3, n, wide)), mem((wide, wide)),
             mem((wide, rank)), mem((wide // 2, rank)), mem((3, n, rank)), mem((wide, rank)),
-            mem((2, wide, cols)), mem((2, wide // 2, cols)), mem((2, 3, n, cols)), mem((2, wide, cols)),
+            mem((2, wide, cols)), mem((2, wide // 2, cols)), mem((2, 6, n // 2, cols)), mem((2, wide, cols)),
             mem((wide, wide)), mem((wide, wide)), mem((wide, wide)),
             mem((136, 256)), mem((8, 256)), mem((136, 8)),
-            mem((4, 3, r1, 128)), mem((4, 3, r1, 128)), mem((4, 3, r2, 128)), mem((4, 3, r2, 128)),
+            mem((4, 6, r1 // 2, 128)), mem((4, 6, r1 // 2, 128)), mem((4, 3, r2, 128)), mem((4, 3, r2, 128)),
             mem((1, 8, 128)), mem((5, 8, 128)), mem((8, rank)), mem((15, 8, rank)),
-            pltpu.SemaphoreType.DMA((17,)), pltpu.SemaphoreType.DMA((6,)),
-            pltpu.SemaphoreType.DMA((160,)), pltpu.SemaphoreType.DMA((160,)),
+            pltpu.SemaphoreType.DMA((17,)), pltpu.SemaphoreType.DMA((10,)),
+            pltpu.SemaphoreType.DMA((208,)), pltpu.SemaphoreType.DMA((208,)),
         ],
         compiler_params=pltpu.CompilerParams(
             collective_id=0, has_side_effects=True, vmem_limit_bytes=62 * 2**20
@@ -519,7 +631,7 @@
     def out(shape, kind=F32):
         return jax.ShapeDtypeStruct(shape, kind)
 
-    oh, ol, bth, btl, back, scale = sums_call(momentum, gradient, basis)
+    oh, ol, bth, btl, back, scale, corrected = sums_call(momentum, gradient, basis)
     tiles = 4
     tr, tc = rows // tiles, cols // tiles
 
@@ -533,11 +645,11 @@
         kernel_outputs,
         grid=(tiles,),
         out_shape=(out((rows, cols)), out((cols, rank)), out((rows, cols), BF16)),
-        in_specs=[rowed(cols), rowed(cols), rowed(rank), rowed(rank), fixed, fixed, cut_cols, small],
+        in_specs=[rowed(cols), rowed(rank), rowed(rank), fixed, fixed, cut_cols, small],
         out_specs=(rowed(cols), cut_cols, rowed(cols)),
         compiler_params=pltpu.CompilerParams(vmem_limit_bytes=62 * 2**20),
         cost_estimate=pl.CostEstimate(flops=4 * 10**9, bytes_accessed=18 * 2**20, transcendentals=0),
-    )(momentum, gradient, oh, ol, bth, btl, back, scale)
+    )(corrected, oh, ol, bth, btl, back, scale)
 
 
 def solution(mesh):

time: 101 us -> 94.9 us (0.940); the launches traced: 100 us -> 93.1 us
  Pallas kernels: 99.7 us -> 92.5 us
    pallas_call x1, Pallas kernels: 90.2 us -> 83.6 us  [sums_call(): pl.pallas_call(kernel_sums, out_shape=tuple((out(*o) for o in outs)) + (r...]
where the time goes in v4:
time: 94.9 us; the launch traced here: 93.1 us
  Pallas kernels  92.5 us (97%)
    pallas_call x1, Pallas kernels, sums_call(): pl.pallas_call(kernel_sums, out_shape=tuple((out(*o) for o in outs)) + (r...  83.6 us
    pallas_call x1, Pallas kernels, shards(): pl.pallas_call(kernel_outputs, grid=(tiles,), out_shape=(out((rows, cols)...  8.88 us

profile of v4, /device:TPU:0, one launch (start us, length us, event | category | flops | bytes accessed | tf_op | source)
XLA Modules:
  0.0 93.1 jit_solution(12797138992411174358)
XLA Ops:
  0.6 83.6 %shard_map.58 = (bf16[1024,512]{1,0:T(8,128)(2,1)}, bf16[1024,512]{1,0:T(8,128)(2,1)}, bf16[512,896]{1,0:T(8,128)(2,1)}, bf16[512,896]{1,0:T(8,128)(2,1)}, f32[8...) custom-call(f32[1024,896]{1,0:T(8,128)} %m_hbm.1, bf16[1024,896]{1,0:T(8,128)(2,1)} %g_hbm.1, f32[896,512]{1,0:T(8,128)} %v_hbm.1), custom_call_target="tpu_custom_call" | custom-call | flops 10000000000 | bytes 20971520 | tf_op jit(solution)/shard_map/pallas_call | solution.py:599
  84.2 8.9 %shard_map.59 = (f32[1024,896]{1,0:T(8,128)}, f32[896,512]{1,0:T(8,128)}, bf16[1024,896]{1,0:T(8,128)(2,1)}) custom-call(f32[1024,896]{1,0:T(8,128)} %get-tuple-element.10.mi_ref, bf16[1024,512]{1,0:T(8,128)(2,1)} %get-tuple-element.11.oh_ref, bf16[1024,512]{1,0:T(8,128)(2,1)} %get-tuple-element.12.ol_ref, bf16[512,896]{1,0:T(8,128)(2,1)} %get-tuple-element.13.bth_ref, ...), custom_call_target="tpu_custom_call" | custom-call | flops 4000000000 | bytes 18874368 | tf_op jit(solution)/shard_map/pallas_call | solution.py:644

commit v5 on v4

--- a/solution.py
+++ b/solution.py
@@ -178,7 +178,7 @@
 
 
 class SumOver8:
-    def __init__(self, links, ring, core, partner, ref, pair, land, total, relay=False):
+    def __init__(self, links, ring, core, partner, ref, pair, land, total, relay=False, relay_back=False):
         self.k, self.core, self.partner, self.ref, self.pair, self.total = links, core, partner, ref, pair, total
         self.ring = ring
         self.n = ref.shape[0] // 2
@@ -186,9 +186,9 @@
         self.s = [links.slot() for _ in range(5)]
         self.base = core * self.n
         self.other = (1 - core) * self.n
-        self.relay = relay
+        self.relay_back = relay_back
         self.reduce = (RelayReduce if relay else Reduce)(links, ring, ref, self.base, self.rows, land)
-        self.gather = (RelayGather if relay else Gather)(links, ring, total, self.base, self.rows)
+        self.gather = (RelayGather if relay_back else Gather)(links, ring, total, self.base, self.rows)
 
     def exchange(self):
         self.k.send(self.s[0], cut(self.ref, self.other, self.n), self.pair, self.partner)
@@ -212,7 +212,7 @@
         self.reduce.mid()
 
     def forward(self):
-        if self.relay:
+        if self.relay_back:
             self.gather.mid()
         else:
             self.last()
@@ -242,22 +242,22 @@
     return terms[0]
 
 
-def eight(s, a_ref, r_ref, t_ref):
+def eight(s, a_ref, d_ref, r_ref, t_ref):
     sid = lax.broadcasted_iota(jnp.int32, (8, 128), 0)
+    lid = lax.broadcasted_iota(jnp.int32, (8, 128), 1) - 8 * s
     o = pl.multiple_of(8 * s, 8)
     on = pl.multiple_of(8 * s + 8, 8)
-    p, q = a_ref[pl.ds(o, 8), 0:128], a_ref[pl.ds(o, 8), 128:256]
-    n, nx = a_ref[pl.ds(on, 8), 0:128], a_ref[pl.ds(on, 8), 128:256]
+    p, n = a_ref[pl.ds(o, 8), :], a_ref[pl.ds(on, 8), :]
     last = r_ref[...]
     t = t_ref[pl.ds(on, 8), :]
-    terms, termsx = [], []
-    for j in range(8):
-        l = jnp.broadcast_to(t[:, j:j + 1], (8, 128))
-        terms.append(l * row(last[:, 0:128], j))
-        termsx.append(l * row(last[:, 128:256], j))
-    n, nx = n - tree(terms), nx - tree(termsx)
+    before = (lid >= -8) & (lid < 0)
+    now = (lid >= 0) & (lid < 8)
+    terms = [jnp.broadcast_to(t[:, j:j + 1], (8, 128)) * row(last, j) for j in range(8)]
+    n = jnp.where(before, 0.0, n) - tree(terms)
     cb = [lane(p, 8 * s + j) for j in range(8)]
     cn = [lane(n, 8 * s + j) for j in range(8)]
+    p = jnp.where(now, jnp.where(lid == sid, 1.0, 0.0), p)
+    n = jnp.where(now, 0.0, n)
     pivot = row(cb[0], 0)
     pivots = pivot
     for j in range(8):
@@ -271,43 +271,38 @@
             m = row(cb[k], j)
             cb[k] = cb[k] - (cm * m) * d
             cn[k] = cn[k] - cn[j] * (m * d)
-        u, ux = row(p, j) * d, row(q, j) * d
-        p, q = p - cm * u, q - cm * ux
-        n, nx = n - cn[j] * u, nx - cn[j] * ux
-    scale = lax.rsqrt(pivots)
-    p, q = p * scale, q * scale
+        u = row(p, j) * d
+        p, n = p - cm * u, n - cn[j] * u
+    p = p * lax.rsqrt(pivots)
     rest = jnp.dot(t_ref[0:128, :], last, precision=HI, preferred_element_type=F32)
-    rid = lax.broadcasted_iota(jnp.int32, (128, 256), 0)
-    a_ref[0:128, :] -= jnp.where(rid >= 8 * s + 16, rest, 0.0)
-    a_ref[pl.ds(o, 8), 128:256] = q
-    a_ref[pl.ds(on, 8), 0:128] = n
-    a_ref[pl.ds(on, 8), 128:256] = nx
-    r_ref[:, 0:128] = p
-    r_ref[:, 128:256] = q
+    lids = lax.broadcasted_iota(jnp.int32, (128, 128), 1) - 8 * s
+    a_ref[0:128, :] = jnp.where((lids >= -8) & (lids < 0), 0.0, a_ref[0:128, :]) - rest
+    a_ref[pl.ds(on, 8), :] = n
+    d_ref[pl.ds(o, 8), :] = p
+    r_ref[...] = p
     t_ref[0:128, :] = p.T
 
 
-def factor_step(k, s_ref, a_ref, r_ref, t_ref, event):
+def factor_step(k, s_ref, a_ref, d_ref, r_ref, t_ref, event):
     n = s_ref.shape[0]
     o = 128 * k
     i128 = lax.broadcasted_iota(jnp.int32, (128, 128), 0)
     j128 = lax.broadcasted_iota(jnp.int32, (128, 128), 1)
     unit = jnp.where(i128 == j128, 1.0, 0.0).astype(F32)
-    a_ref[0:128, 0:128] = s_ref[o:o + 128, o:o + 128]
-    a_ref[0:128, 128:256] = unit
-    a_ref[128:136, :] = jnp.zeros((8, 256), F32)
+    a_ref[0:128, :] = s_ref[o:o + 128, o:o + 128]
+    a_ref[128:136, :] = jnp.zeros((8, 128), F32)
     r_ref[...] = jnp.zeros(r_ref.shape, F32)
     t_ref[...] = jnp.zeros(t_ref.shape, F32)
 
     def body(s, c):
-        eight(s, a_ref, r_ref, t_ref)
+        eight(s, a_ref, d_ref, r_ref, t_ref)
         return c
 
     for quarter in range(4):
         lax.fori_loop(4 * quarter, 4 * quarter + 4, body, 0)
         event()
     s_ref[o:o + 128, o:o + 128] = unit
-    block = jnp.dot(a_ref[0:128, 128:256], s_ref[o:o + 128, :], precision=HI, preferred_element_type=F32)
+    block = jnp.dot(jnp.where(j128 <= i128, d_ref[...], 0.0), s_ref[o:o + 128, :], precision=HI, preferred_element_type=F32)
     s_ref[o:o + 128, :] = block
     if o + 128 < n:
         s_ref[o + 128:, o:o + 128] = jnp.zeros((n - o - 128, 128), F32)
@@ -326,7 +321,7 @@
     m_ref, g_ref, v_ref, oh_ref, ol_ref, bth_ref, btl_ref, basis_ref, sc_ref,
     bh, bl, vh, vl, part, proj, ph, pl_, pth, ptl,
     gram0, gpair0, gland0, gsum0, gram1, gpair1, gland1, gsum1, w, wpair, wland, wsum,
-    s0, s1, s2, a_ref, r_ref, t_ref, x1, y1, y2, x2, tbuf, tland, colsum, cland,
+    s0, s1, s2, a_ref, d_ref, r_ref, t_ref, x1, y1, y2, x2, tbuf, tland, colsum, cland,
     in_sem, out_sem, send_sem, recv_sem,
 ):
     f, t = lax.axis_index("fsdp"), lax.axis_index("tp")
@@ -373,7 +368,7 @@
         first.append((RelayReduce(links, rx, pq, 0, r1, x1.at[q]), RelayReduce(links, ry, pq, half, r1, y1.at[q])))
         second.append((Reduce(links, ry, pq, base_a, r2, y2.at[q]), Reduce(links, rx, pq, base_b, r2, x2.at[q])))
         third.append((Gather(links, ry, fq, base_a, r2), Gather(links, rx, fq, base_b, r2)))
-        fourth.append((RelayGather(links, rx, fq, 0, r1), RelayGather(links, ry, fq, half, r1)))
+        fourth.append((Gather(links, rx, fq, 0, r1), Gather(links, ry, fq, half, r1)))
 
     def add(q):
         for one in first[q]:
@@ -426,8 +421,7 @@
             four.start()
 
     def step4(q):
-        for four in fourth[q]:
-            four.mid()
+        pass
 
     add(2)
     add(3)
@@ -438,7 +432,7 @@
     g0 = SumOver8(links, rz, core, partner, gram0, gpair0, gland0, gsum0)
     g1 = SumOver8(links, rz, core, partner, gram1, gpair1, gland1, gsum1)
     ws = [
-        SumOver8(links, rz, core, partner, w.at[h], wpair.at[h], wland.at[h], wsum.at[h], True) for h in range(2)
+        SumOver8(links, rz, core, partner, w.at[h], wpair.at[h], wland.at[h], wsum.at[h], True, h == 0) for h in range(2)
     ]
 
     def turned(q):
@@ -465,8 +459,12 @@
     squares = squares + turned(1)
     gram0[...] = dot3(pth[:wide, :], ptl[:wide, :], ph[:, :wide], pl_[:, :wide])
     g0.exchange()
+    products(0, 0)
+    g0.begin()
+    products(0, 1)
+    ws[0].exchange()
     squares = squares + turned(2)
-    g0.begin()
+    ws[0].begin()
     squares = squares + turned(3)
     tbuf[0] = squares
     tslots = [links.slot() for _ in range(4)]
@@ -478,14 +476,12 @@
     for j in range(3):
         links.send(tslots[1 + j], tland.at[z], tland.at[z], rz.devices[j])
     g0.turn()
-    products(0, 0)
+    products(1, 0)
     g1.begin()
-    products(0, 1)
-    ws[0].exchange()
-    products(1, 0)
-    ws[0].begin()
     products(1, 1)
     ws[1].exchange()
+    ws[0].mid()
+    ws[1].begin()
     g0.forward()
     for j in range(3):
         links.landed(tslots[1 + j], tland.at[rz.sources[j]], rz.devices[j])
@@ -495,8 +491,8 @@
     rid = lax.broadcasted_iota(jnp.int32, (wide, wide), 0)
     cid = lax.broadcasted_iota(jnp.int32, (wide, wide), 1)
     diagonal = jnp.where(rid == cid, shift, 0.0)
-    events = [g1.turn, ws[0].mid, ws[1].begin, None, g1.forward, ws[0].turn, g1.end, ws[1].mid,
-              ws[0].forward, ws[1].turn, None, ws[0].last, None, ws[1].forward, None, None]
+    events = [None, g1.turn, ws[0].turn, None, ws[1].mid, None, g1.forward, g1.end,
+              ws[0].forward, ws[1].turn, None, None, ws[0].last, None, None, ws[0].end]
 
     def event():
         e = events.pop(0)
@@ -505,30 +501,29 @@
 
     s0[...] = gsum0[...] + diagonal
     for k in range(wide // 128):
-        factor_step(k, s0, a_ref, r_ref, t_ref, event)
+        factor_step(k, s0, a_ref, d_ref, r_ref, t_ref, event)
     inv0 = jnp.where(cid <= rid, s0[...], 0.0)
     s0[...] = inv0
     low = full(gsum1[:, :wide], inv0, NT)
     s1[...] = gsum1[:, wide:] + diagonal - full(low, low, NT)
     s2[...] = full(low, inv0)
     for k in range(wide // 128):
-        factor_step(k, s1, a_ref, r_ref, t_ref, event)
+        factor_step(k, s1, a_ref, d_ref, r_ref, t_ref, event)
     inv1 = jnp.where(cid <= rid, s1[...], 0.0)
     x0h, x0l = split(s0[...])
     x1h, x1l = split(inv1)
     xch, xcl = split(-full(inv1, s2[...]))
-    ws[1].last()
-    ws[0].end()
-    ws[1].end()
 
     w0h, w0l = split(wsum[0])
-    w1h, w1l = split(wsum[1])
     sums = []
     for h in range(2):
         col = slice(h * wide, (h + 1) * wide)
         if h == 0:
             back_t = dot3(x0h, x0l, w0h, w0l)
         else:
+            ws[1].forward()
+            ws[1].end()
+            w1h, w1l = split(wsum[1])
             back_t = dot3(xch, xcl, w0h, w0l) + dot3(x1h, x1l, w1h, w1l)
         bth_ref[col, :], btl_ref[col, :] = split(back_t)
         back = back_t.T
@@ -611,7 +606,7 @@
             mem((wide, rank)), mem((wide // 2, rank)), mem((3, n, rank)), mem((wide, rank)),
             mem((2, wide, cols)), mem((2, wide // 2, cols)), mem((2, 6, n // 2, cols)), mem((2, wide, cols)),
             mem((wide, wide)), mem((wide, wide)), mem((wide, wide)),
-            mem((136, 256)), mem((8, 256)), mem((136, 8)),
+            mem((136, 128)), mem((128, 128)), mem((8, 128)), mem((136, 8)),
             mem((4, 6, r1 // 2, 128)), mem((4, 6, r1 // 2, 128)), mem((4, 3, r2, 128)), mem((4, 3, r2, 128)),
             mem((1, 8, 128)), mem((5, 8, 128)), mem((8, rank)), mem((15, 8, rank)),
             pltpu.SemaphoreType.DMA((17,)), pltpu.SemaphoreType.DMA((10,)),
@@ -632,7 +627,7 @@
         return jax.ShapeDtypeStruct(shape, kind)
 
     oh, ol, bth, btl, back, scale, corrected = sums_call(momentum, gradient, basis)
-    tiles = 4
+    tiles = 2
     tr, tc = rows // tiles, cols // tiles
 
     def rowed(width):

time: 94.9 us -> 93.9 us (0.989); the launches traced: 93.1 us -> 93.5 us
  no operation moved by 1% of the time
where the time goes in v5:
time: 93.9 us; the launch traced here: 93.5 us
  Pallas kernels  92.8 us (99%)
    pallas_call x1, Pallas kernels, sums_call(): pl.pallas_call(kernel_sums, out_shape=tuple((out(*o) for o in outs)) + (r...  84.4 us
    pallas_call x1, Pallas kernels, shards(): pl.pallas_call(kernel_outputs, grid=(tiles,), out_shape=(out((rows, cols)...  8.39 us

profile of v5, /device:TPU:0, one launch (start us, length us, event | category | flops | bytes accessed | tf_op | source)
XLA Modules:
  0.0 93.5 jit_solution(9232038355972098898)
XLA Ops:
  0.6 84.4 %shard_map.58 = (bf16[1024,512]{1,0:T(8,128)(2,1)}, bf16[1024,512]{1,0:T(8,128)(2,1)}, bf16[512,896]{1,0:T(8,128)(2,1)}, bf16[512,896]{1,0:T(8,128)(2,1)}, f32[8...) custom-call(f32[1024,896]{1,0:T(8,128)} %m_hbm.1, bf16[1024,896]{1,0:T(8,128)(2,1)} %g_hbm.1, f32[896,512]{1,0:T(8,128)} %v_hbm.1), custom_call_target="tpu_custom_call" | custom-call | flops 10000000000 | bytes 20971520 | tf_op jit(solution)/shard_map/pallas_call | solution.py:594
  85.1 8.4 %shard_map.59 = (f32[1024,896]{1,0:T(8,128)}, f32[896,512]{1,0:T(8,128)}, bf16[1024,896]{1,0:T(8,128)(2,1)}) custom-call(f32[1024,896]{1,0:T(8,128)} %get-tuple-element.10.mi_ref, bf16[1024,512]{1,0:T(8,128)(2,1)} %get-tuple-element.11.oh_ref, bf16[1024,512]{1,0:T(8,128)(2,1)} %get-tuple-element.12.ol_ref, bf16[512,896]{1,0:T(8,128)(2,1)} %get-tuple-element.13.bth_ref, ...), custom_call_target="tpu_custom_call" | custom-call | flops 4000000000 | bytes 18874368 | tf_op jit(solution)/shard_map/pallas_call | solution.py:639
